TPU v7x, 256 devices: a whole 4x4x8 slice. The times are simulated.
256 devices in a mesh: ep: 64 (over z, x, core), tp: 4 (over y).
Axes of the slice: x: 4, y: 4, z: 8, core: 2. Of those that a mesh axis runs over, the one named last changes fastest.
Arguments:
- features: bfloat16 [16384, 1024], P('ep'), may hold values from -6 to 6
- cotangent: bfloat16 [16384, 2048], P('ep'), may hold values from -6 to 6
- expert_ids: int32 [16384, 2], P('ep'), may hold values from 0 to 7, all different within a row; in each aligned block of 32 rows (0 to 31, 32 to 63, ...) at most 12 rows name the same one
- gate_levels: int32 [16384, 2], P('ep'), may hold values from 1 to 15
- w_in: bfloat16 [64, 1024, 512], P('ep', None, 'tp'), may hold values from -0.1875 to 0.1875
- w_out: bfloat16 [64, 512, 2048], P('ep', 'tp'), may hold values from -0.09375 to 0.09375
Outputs:
- grad_in: bfloat16 [16384, 1024], P('ep', 'tp')
- grad_w_in: bfloat16 [64, 1024, 512], P('ep', None, 'tp')
- grad_w_out: bfloat16 [64, 512, 2048], P('ep', 'tp')
Inputs may be any that keep to these rules, and one draw needn't show every extreme that they name: `expert_ids`: each row names two different experts. In each aligned block of 32 rows no expert is named by more than 12 rows, and some expert reaches 12 rows in some block.
All inputs are finite; a program needn't handle non-finite values.
Results may differ from a plain program's by a relative error of at most 0.0065.
Values may be sent and summed in bfloat16 or wider, within the bound.
A program may use at most 128 MiB of HBM per device.

v0:
```python
import math

import jax
import jax.numpy as jnp
from jax import lax
from jax.sharding import PartitionSpec as P

E = 8


def shifted(value, axis, by):
    peers = lax.axis_size(axis)
    return lax.ppermute(value, axis, [(i, (i + by) % peers) for i in range(peers)])


def slot_positions(expert_ids, blocks, experts, capacity):
    flattened = expert_ids.reshape(blocks, -1)
    one_hot = (flattened[:, :, None] == jnp.arange(experts, dtype=jnp.int32)[None, None, :]).astype(
        jnp.int32
    )
    earlier = jnp.cumsum(one_hot, axis=1) - one_hot
    within = jnp.sum(one_hot * earlier, axis=2)
    block_ids = jnp.arange(blocks, dtype=jnp.int32)[:, None]
    return ((block_ids * experts + flattened) * capacity + within).reshape(-1)


def shards(features, cotangent, expert_ids, gate_levels, w_in, w_out):
    device_count = lax.axis_size("ep")
    replicas = device_count // E
    replica = lax.axis_index("ep") // E
    tokens_here = expert_ids.shape[0]
    sub_rows = tokens_here // replicas
    capacity = 3 * sub_rows // 8
    slot_count = device_count * capacity
    pair_count = 2 * tokens_here
    positions = slot_positions(expert_ids, replicas, E, capacity)
    owner = (
        jnp.full((slot_count,), pair_count, jnp.int32)
        .at[positions]
        .set(jnp.arange(pair_count, dtype=jnp.int32))
    )
    filled = owner < pair_count
    pair_ids = jnp.minimum(owner, pair_count - 1)
    token_ids = pair_ids // 2
    gate_values = gate_levels.reshape(-1).astype(jnp.float32) / 16.0
    slot_gates = jnp.where(filled, gate_values[pair_ids], 0.0)
    slot_mask = filled.astype(jnp.bfloat16)[:, None]
    packed_x = features[token_ids] * slot_mask
    packed_dy = (cotangent[token_ids].astype(jnp.float32) * slot_gates[:, None]).astype(
        jnp.bfloat16
    )
    rows_x, rows_dy = (
        lax.all_to_all(packed_x, "ep", split_axis=0, concat_axis=0, tiled=True),
        lax.all_to_all(packed_dy, "ep", split_axis=0, concat_axis=0, tiled=True),
    )
    piece_in = w_in[0]
    piece_out = w_out[0]
    span = piece_in.shape[1]
    weight_in = jnp.zeros((piece_in.shape[0], span * replicas), jnp.bfloat16)
    weight_out = jnp.zeros((span * replicas, piece_out.shape[1]), jnp.bfloat16)
    weight_in = lax.dynamic_update_slice_in_dim(weight_in, piece_in, replica * span, 1)
    weight_out = lax.dynamic_update_slice_in_dim(weight_out, piece_out, replica * span, 0)
    moving = (piece_in, piece_out)
    for turn_index in range(1, replicas):
        moving = shifted((moving[0], moving[1]), "ep", E)
        anchor = (replica - turn_index) % replicas
        weight_in = lax.dynamic_update_slice_in_dim(weight_in, moving[0], anchor * span, 1)
        weight_out = lax.dynamic_update_slice_in_dim(weight_out, moving[1], anchor * span, 0)
    pre = jnp.dot(rows_x, weight_in, preferred_element_type=jnp.float32)
    activated, gelu_back = jax.vjp(jax.nn.gelu, pre)
    act_rows = activated.astype(jnp.bfloat16)
    back_act = lax.dot_general(
        rows_dy, weight_out, (((1,), (1,)), ((), ())), preferred_element_type=jnp.float32
    )
    back_pre = gelu_back(back_act)[0].astype(jnp.bfloat16)
    summed = lax.psum_scatter(
        lax.dot_general(
            weight_in, back_pre, (((1,), (1,)), ((), ())), preferred_element_type=jnp.float32
        ),
        "tp",
        scatter_dimension=0,
        tiled=True,
    )
    returned = lax.all_to_all(
        summed.astype(jnp.bfloat16), "ep", split_axis=1, concat_axis=1, tiled=True
    )
    picked = returned[:, positions].astype(jnp.float32)
    grad_in = jnp.sum(picked.reshape(picked.shape[0], tokens_here, 2), axis=2).T.astype(
        jnp.bfloat16
    )

    def span_grads(first_span, span_total):
        width = span_total * span
        act_cols = lax.dynamic_slice_in_dim(act_rows, first_span * span, width, 1)
        pre_cols = lax.dynamic_slice_in_dim(back_pre, first_span * span, width, 1)
        grad_first = lax.dot_general(
            pre_cols, rows_x, (((0,), (0,)), ((), ())), preferred_element_type=jnp.float32
        )
        grad_second = lax.dot_general(
            act_cols, rows_dy, (((0,), (0,)), ((), ())), preferred_element_type=jnp.float32
        )
        return (grad_first, grad_second)

    summed_grads = span_grads((replica - 1) % replicas, 1)
    for turn_index in range(1, replicas):
        summed_grads = shifted((summed_grads[0], summed_grads[1]), "ep", E)
        own_grads = span_grads((replica - turn_index - 1) % replicas, 1)
        summed_grads = (summed_grads[0] + own_grads[0], summed_grads[1] + own_grads[1])
    grad_scale = 1.0 / math.sqrt(2.0 * tokens_here * device_count / E)
    grad_w_in = (summed_grads[0] * grad_scale).T.astype(jnp.bfloat16)[None]
    grad_w_out = (summed_grads[1] * grad_scale).astype(jnp.bfloat16)[None]
    return (grad_in, grad_w_in, grad_w_out)


def solution(mesh):
    return jax.shard_map(
        shards,
        mesh=mesh,
        in_specs=(
            P("ep", None),
            P("ep", None),
            P("ep", None),
            P("ep", None),
            P("ep", None, "tp"),
            P("ep", "tp", None),
        ),
        out_specs=(P("ep", "tp"), P("ep", None, "tp"), P("ep", "tp", None)),
        check_vma=False,
    )
```

profile of v0, /device:TPU:1, one launch (start us, length us, event | category | flops | bytes accessed | tf_op | source)
XLA Modules:
  0.0 600.0 jit_solution(11202077392058330161)
XLA Ops:
  7.2 0.9 copy.23
  8.4 1.4 fusion.62
  10.1 2.4 scatter_custom_fusion
  13.6 5.0 gather_fusion.1
  18.7 3.5 gather_fusion.2
  22.2 2.4 gather.17
  24.7 1.5 broadcast_multiply_fusion
  26.2 13.0 %all-to-all-start.1 = ((bf16[64,12,1024]{2,1,0:T(8,128)(2,1)}), bf16[64,12,1024]{2,1,0:T(8,128)(2,1)S(1)}, u32[]{:S(2)}, u32[]{:S(2)}) async-start(bf16[64,12,1024]{2,1,0:T(8,128)(2,1)} %broadcast_multiply_fusion), calls=%async_computation.1 | async-start | bytes 4194304 | tf_op jit(solution)/shard_map/all_to_all | solution.py:53
  39.2 4.2 gather_fusion
  43.5 6.5 %reshape.90 = f32[64,12,2048]{2,1,0:T(8,128)} reshape(bf16[768,2048]{1,0:T(8,128)(2,1)} %gather_fusion) | data formatting | bytes 9437184 | tf_op jit(solution)/shard_map/convert_element_type | solution.py:49
  50.0 5.9 multiply_convert_fusion
  56.0 32.9 %all-to-all-done.1 = bf16[64,12,1024]{2,1,0:T(8,128)(2,1)S(1)} async-done(((bf16[64,12,1024]{2,1,0:T(8,128)(2,1)}), bf16[64,12,1024]{2,1,0:T(8,128)(2,1)S(1)}, u32[]{:S(2)}, u32[]{:S(2)}) %all-to-all-start.1) | async-done | bytes 1572896 | tf_op jit(solution)/shard_map/all_to_all | solution.py:53
  88.9 7.2 %all-to-all-start = ((bf16[64,12,2048]{2,1,0:T(8,128)(2,1)}), bf16[64,12,2048]{2,1,0:T(8,128)(2,1)}, u32[]{:S(2)}, u32[]{:S(2)}) async-start(bf16[64,12,2048]{2,1,0:T(8,128)(2,1)} %multiply_convert_fusion), calls=%async_computation | async-start | bytes 8388608 | tf_op jit(solution)/shard_map/all_to_all | solution.py:54
  96.2 1.5 collective-permute-start.7
  97.6 102.9 %collective-permute-done.7 = bf16[128,2048]{1,0:T(8,128)(2,1)S(1)} collective-permute-done((bf16[128,2048]{1,0:T(8,128)(2,1)S(1)}, bf16[128,2048]{1,0:T(8,128)(2,1)S(1)}, u32[]{:S(2)}, u32[]{:S(2)}) %collective-permute-start.7) | collective-permute-done | bytes 524320 | tf_op jit(solution)/shard_map/ppermute | solution.py:13
  200.7 19.4 %collective-permute-done = bf16[1024,128]{1,0:T(8,128)(2,1)} collective-permute-done((bf16[1024,128]{1,0:T(8,128)(2,1)S(1)}, bf16[1024,128]{1,0:T(8,128)(2,1)}, u32[]{:S(2)}, u32[]{:S(2)}) %collective-permute-start) | collective-permute-done | bytes 262176 | tf_op jit(solution)/shard_map/ppermute | solution.py:13
  220.9 6.8 %collective-permute-done.1 = bf16[1024,128]{1,0:T(8,128)(2,1)} collective-permute-done((bf16[1024,128]{1,0:T(8,128)(2,1)}, bf16[1024,128]{1,0:T(8,128)(2,1)}, u32[]{:S(2)}, u32[]{:S(2)}) %collective-permute-start.1) | collective-permute-done | bytes 262176 | tf_op jit(solution)/shard_map/ppermute | solution.py:13
  227.6 2.6 broadcast_in_dim.33
  231.0 13.4 %collective-permute-done.2 = bf16[1024,128]{1,0:T(8,128)(2,1)S(1)} collective-permute-done((bf16[1024,128]{1,0:T(8,128)(2,1)}, bf16[1024,128]{1,0:T(8,128)(2,1)S(1)}, u32[]{:S(2)}, u32[]{:S(2)}) %collective-permute-start.2) | collective-permute-done | bytes 262176 | tf_op jit(solution)/shard_map/ppermute | solution.py:13
  244.4 1.6 broadcast_in_dim.29
  246.8 1.7 constant_dynamic-update-slice_fusion.14
  248.5 2.4 collective-permute-done.3
  251.7 10.2 %collective-permute-done.10 = bf16[128,2048]{1,0:T(8,128)(2,1)S(1)} collective-permute-done((bf16[128,2048]{1,0:T(8,128)(2,1)S(1)}, bf16[128,2048]{1,0:T(8,128)(2,1)S(1)}, u32[]{:S(2)}, u32[]{:S(2)}) %collective-permute-start.10) | collective-permute-done | bytes 524320 | tf_op jit(solution)/shard_map/ppermute | solution.py:13
  261.9 1.7 constant_dynamic-update-slice_fusion.13
  264.4 3.2 collective-permute-done.4
  267.6 1.9 constant_dynamic-update-slice_fusion.5
  270.2 8.6 %collective-permute-done.11 = bf16[128,2048]{1,0:T(8,128)(2,1)S(1)} collective-permute-done((bf16[128,2048]{1,0:T(8,128)(2,1)S(1)}, bf16[128,2048]{1,0:T(8,128)(2,1)S(1)}, u32[]{:S(2)}, u32[]{:S(2)}) %collective-permute-start.11) | collective-permute-done | bytes 524320 | tf_op jit(solution)/shard_map/ppermute | solution.py:13
  279.5 4.9 collective-permute-done.5
  286.0 15.3 %collective-permute-done.6 = bf16[1024,128]{1,0:T(8,128)(2,1)S(1)} collective-permute-done((bf16[1024,128]{1,0:T(8,128)(2,1)S(1)}, bf16[1024,128]{1,0:T(8,128)(2,1)S(1)}, u32[]{:S(2)}, u32[]{:S(2)}) %collective-permute-start.6) | collective-permute-done | bytes 262176 | tf_op jit(solution)/shard_map/ppermute | solution.py:13
  303.9 1.3 all_to_all.23
  306.0 7.2 %collective-permute-done.13 = bf16[128,2048]{1,0:T(8,128)(2,1)S(1)} collective-permute-done((bf16[128,2048]{1,0:T(8,128)(2,1)S(1)}, bf16[128,2048]{1,0:T(8,128)(2,1)S(1)}, u32[]{:S(2)}, u32[]{:S(2)}) %collective-permute-start.13) | collective-permute-done | bytes 524320 | tf_op jit(solution)/shard_map/ppermute | solution.py:13
  314.0 4.7 all_to_all.21
  318.8 5.4 fusion.63
  324.2 5.5 multiply_convert_fusion.1
  329.7 1.9 fusion.24
  331.7 5.1 fusion.64
  336.8 16.5 %collective-permute-done.21 = f32[128,2048]{1,0:T(8,128)} collective-permute-done((f32[128,2048]{1,0:T(8,128)}, f32[128,2048]{1,0:T(8,128)}, u32[]{:S(2)}, u32[]{:S(2)}) %collective-permute-start.21) | collective-permute-done | bytes 1048608 | tf_op jit(solution)/shard_map/ppermute | solution.py:13
  353.3 2.0 convolution_add_fusion
  356.0 19.8 %collective-permute-done.22 = f32[128,2048]{1,0:T(8,128)S(1)} collective-permute-done((f32[128,2048]{1,0:T(8,128)S(1)}, f32[128,2048]{1,0:T(8,128)S(1)}, u32[]{:S(2)}, u32[]{:S(2)}) %collective-permute-start.22) | collective-permute-done | bytes 1048608 | tf_op jit(solution)/shard_map/ppermute | solution.py:13
  377.2 20.2 %collective-permute-done.23 = f32[128,2048]{1,0:T(8,128)S(1)} collective-permute-done((f32[128,2048]{1,0:T(8,128)S(1)}, f32[128,2048]{1,0:T(8,128)S(1)}, u32[]{:S(2)}, u32[]{:S(2)}) %collective-permute-start.23) | collective-permute-done | bytes 1048608 | tf_op jit(solution)/shard_map/ppermute | solution.py:13
  397.9 10.8 %collective-permute-done.14 = f32[128,1024]{1,0:T(8,128)S(1)} collective-permute-done((f32[128,1024]{1,0:T(8,128)S(1)}, f32[128,1024]{1,0:T(8,128)S(1)}, u32[]{:S(2)}, u32[]{:S(2)}) %collective-permute-start.14) | collective-permute-done | bytes 524320 | tf_op jit(solution)/shard_map/ppermute | solution.py:13
  409.8 21.3 %collective-permute-done.24 = f32[128,2048]{1,0:T(8,128)S(1)} collective-permute-done((f32[128,2048]{1,0:T(8,128)S(1)}, f32[128,2048]{1,0:T(8,128)S(1)}, u32[]{:S(2)}, u32[]{:S(2)}) %collective-permute-start.24) | collective-permute-done | bytes 1048608 | tf_op jit(solution)/shard_map/ppermute | solution.py:13
  431.8 10.6 %collective-permute-done.15 = f32[128,1024]{1,0:T(8,128)S(1)} collective-permute-done((f32[128,1024]{1,0:T(8,128)S(1)}, f32[128,1024]{1,0:T(8,128)S(1)}, u32[]{:S(2)}, u32[]{:S(2)}) %collective-permute-start.15) | collective-permute-done | bytes 524320 | tf_op jit(solution)/shard_map/ppermute | solution.py:13
  443.0 33.1 %collective-permute-done.16 = f32[128,1024]{1,0:T(8,128)S(1)} collective-permute-done((f32[128,1024]{1,0:T(8,128)S(1)}, f32[128,1024]{1,0:T(8,128)S(1)}, u32[]{:S(2)}, u32[]{:S(2)}) %collective-permute-start.16) | collective-permute-done | bytes 524320 | tf_op jit(solution)/shard_map/ppermute | solution.py:13
  476.9 1.1 add.247
  478.4 9.7 %collective-permute-done.17 = f32[128,1024]{1,0:T(8,128)S(1)} collective-permute-done((f32[128,1024]{1,0:T(8,128)S(1)}, f32[128,1024]{1,0:T(8,128)S(1)}, u32[]{:S(2)}, u32[]{:S(2)}) %collective-permute-start.17) | collective-permute-done | bytes 524320 | tf_op jit(solution)/shard_map/ppermute | solution.py:13
  489.0 1.9 fusion.30
  491.0 29.3 %collective-permute-done.18 = f32[128,1024]{1,0:T(8,128)} collective-permute-done((f32[128,1024]{1,0:T(8,128)}, f32[128,1024]{1,0:T(8,128)}, u32[]{:S(2)}, u32[]{:S(2)}) %collective-permute-start.18) | collective-permute-done | bytes 524320 | tf_op jit(solution)/shard_map/ppermute | solution.py:13
  520.3 1.1 add.238
  521.5 1.5 fusion.13
  523.1 2.4 add.248
  525.5 1.3 fusion.28
  526.9 6.2 %collective-permute-done.19 = f32[128,1024]{1,0:T(8,128)S(1)} collective-permute-done((f32[128,1024]{1,0:T(8,128)S(1)}, f32[128,1024]{1,0:T(8,128)S(1)}, u32[]{:S(2)}, u32[]{:S(2)}) %collective-permute-start.19) | collective-permute-done | bytes 524320 | tf_op jit(solution)/shard_map/ppermute | solution.py:13
  534.0 1.9 convert_element_type.56
  535.9 1.2 copy.28
  538.0 22.8 %all-to-all-start.2 = ((bf16[256,64,12]{0,2,1:T(8,128)(2,1)}), bf16[256,64,12]{0,2,1:T(8,128)(2,1)}, u32[]{:S(2)}, u32[]{:S(2)}) async-start(bf16[256,64,12]{0,2,1:T(8,128)(2,1)} %all_to_all.24), calls=%async_computation.3 | async-start | bytes 1048576 | tf_op jit(solution)/shard_map/all_to_all | solution.py:84
  560.8 1.9 fusion.26
  562.7 2.6 fusion.11
  565.3 1.1 fusion.9
  567.2 18.8 %all-to-all-done.2 = bf16[256,64,12]{0,2,1:T(8,128)(2,1)} async-done(((bf16[256,64,12]{0,2,1:T(8,128)(2,1)}), bf16[256,64,12]{0,2,1:T(8,128)(2,1)}, u32[]{:S(2)}, u32[]{:S(2)}) %all-to-all-start.2) | async-done | bytes 393248 | tf_op jit(solution)/shard_map/all_to_all | solution.py:84
  586.1 1.1 all_to_all.26
  587.2 2.0 gather_fusion.3
  589.3 1.3 reduce
  590.6 2.1 fusion.8
  (120 shorter events, 22.9 us)
Async XLA Ops:
  7.2 32.1 %copy-start = (bf16[256,2048]{1,0:T(8,128)(2,1)S(1)}, bf16[256,2048]{1,0:T(8,128)(2,1)}, u32[]{:S(2)}) copy-start(bf16[256,2048]{1,0:T(8,128)(2,1)} %param.7) | copy-start | bytes 3145732
  13.6 5.0 copy-start.2
  26.2 62.7 %all-to-all-start.1 = ((bf16[64,12,1024]{2,1,0:T(8,128)(2,1)}), bf16[64,12,1024]{2,1,0:T(8,128)(2,1)S(1)}, u32[]{:S(2)}, u32[]{:S(2)}) async-start(bf16[64,12,1024]{2,1,0:T(8,128)(2,1)} %broadcast_multiply_fusion), calls=%async_computation.1 | async-start | bytes 4194304 | tf_op jit(solution)/shard_map/all_to_all | solution.py:53
  56.0 40.2 %copy-start.11 = (bf16[1,128,2048]{2,1,0:T(8,128)(2,1)S(1)}, bf16[1,128,2048]{2,1,0:T(8,128)(2,1)}, u32[]{:S(2)}) copy-start(bf16[1,128,2048]{2,1,0:T(8,128)(2,1)} %param.11) | copy-start | bytes 1572868
  56.0 144.6 %copy-start.14 = (bf16[1,1024,128]{2,1,0:T(8,128)(2,1)S(1)}, bf16[1,1024,128]{2,1,0:T(8,128)(2,1)}, u32[]{:S(2)}) copy-start(bf16[1,1024,128]{2,1,0:T(8,128)(2,1)} %param.10) | copy-start | bytes 786436
  88.9 225.1 %all-to-all-start = ((bf16[64,12,2048]{2,1,0:T(8,128)(2,1)}), bf16[64,12,2048]{2,1,0:T(8,128)(2,1)}, u32[]{:S(2)}, u32[]{:S(2)}) async-start(bf16[64,12,2048]{2,1,0:T(8,128)(2,1)} %multiply_convert_fusion), calls=%async_computation | async-start | bytes 8388608 | tf_op jit(solution)/shard_map/all_to_all | solution.py:54
  96.1 437.9 %reduce-scatter.2.cloned.1.call-start = ((), (), s32[]{:S(2)}) async-start(), calls=%async_computation.4 | async-start | bytes 3932160 | tf_op jit(solution)/shard_map/reduce_scatter | solution.py:76
  96.2 104.4 %collective-permute-start.7 = (bf16[128,2048]{1,0:T(8,128)(2,1)S(1)}, bf16[128,2048]{1,0:T(8,128)(2,1)S(1)}, u32[]{:S(2)}, u32[]{:S(2)}) collective-permute-start(bf16[128,2048]{1,0:T(8,128)(2,1)S(1)} %bitcast.42), channel_id=1, source_target_pairs={{0,32},{4,36},{8,40},{12,44},{16,48},{20,52},{24,56},{28,60},{32,6... | collective-permute-start | bytes 1572872 | tf_op jit(solution)/shard_map/ppermute | solution.py:13
  200.6 19.5 %copy-start.12 = (bf16[128,2048]{1,0:T(8,128)(2,1)}, bf16[128,2048]{1,0:T(8,128)(2,1)S(1)}, u32[]{:S(2)}) copy-start(bf16[128,2048]{1,0:T(8,128)(2,1)S(1)} %collective-permute-done.7) | copy-start | bytes 1572868
  200.6 19.5 %collective-permute-start.8 = (bf16[128,2048]{1,0:T(8,128)(2,1)S(1)}, bf16[128,2048]{1,0:T(8,128)(2,1)}, u32[]{:S(2)}, u32[]{:S(2)}) collective-permute-start(bf16[128,2048]{1,0:T(8,128)(2,1)S(1)} %collective-permute-done.7), channel_id=1, source_target_pairs={{0,32},{4,36},{8,40},{12,44},{16,48},{20,52},{24,56},{28,60},{32,6... | collective-permute-start | bytes 1572872 | tf_op jit(solution)/shard_map/ppermute | solution.py:13
  200.6 19.5 %collective-permute-start = (bf16[1024,128]{1,0:T(8,128)(2,1)S(1)}, bf16[1024,128]{1,0:T(8,128)(2,1)}, u32[]{:S(2)}, u32[]{:S(2)}) collective-permute-start(bf16[1024,128]{1,0:T(8,128)(2,1)S(1)} %bitcast.43), channel_id=1, source_target_pairs={{0,32},{4,36},{8,40},{12,44},{16,48},{20,52},{24,56},{28,60},{32,6... | collective-permute-start | bytes 786440 | tf_op jit(solution)/shard_map/ppermute | solution.py:13
  220.1 7.6 %collective-permute-start.1 = (bf16[1024,128]{1,0:T(8,128)(2,1)}, bf16[1024,128]{1,0:T(8,128)(2,1)}, u32[]{:S(2)}, u32[]{:S(2)}) collective-permute-start(bf16[1024,128]{1,0:T(8,128)(2,1)} %collective-permute-done), channel_id=1, source_target_pairs={{0,32},{4,36},{8,40},{12,44},{16,48},{20,52},{24,56},{28,60},{32,6... | collective-permute-start | bytes 786440 | tf_op jit(solution)/shard_map/ppermute | solution.py:13
  220.1 24.3 %collective-permute-start.9 = (bf16[128,2048]{1,0:T(8,128)(2,1)}, bf16[128,2048]{1,0:T(8,128)(2,1)S(1)}, u32[]{:S(2)}, u32[]{:S(2)}) collective-permute-start(bf16[128,2048]{1,0:T(8,128)(2,1)} %collective-permute-done.8), channel_id=1, source_target_pairs={{0,32},{4,36},{8,40},{12,44},{16,48},{20,52},{24,56},{28,60},{32,6... | collective-permute-start | bytes 1572872 | tf_op jit(solution)/shard_map/ppermute | solution.py:13
  227.6 16.7 %collective-permute-start.2 = (bf16[1024,128]{1,0:T(8,128)(2,1)}, bf16[1024,128]{1,0:T(8,128)(2,1)S(1)}, u32[]{:S(2)}, u32[]{:S(2)}) collective-permute-start(bf16[1024,128]{1,0:T(8,128)(2,1)} %collective-permute-done.1), channel_id=1, source_target_pairs={{0,32},{4,36},{8,40},{12,44},{16,48},{20,52},{24,56},{28,60},{32,6... | collective-permute-start | bytes 786440 | tf_op jit(solution)/shard_map/ppermute | solution.py:13
  230.2 20.6 %copy-start.13 = (bf16[128,2048]{1,0:T(8,128)(2,1)S(1)}, bf16[128,2048]{1,0:T(8,128)(2,1)}, u32[]{:S(2)}) copy-start(bf16[128,2048]{1,0:T(8,128)(2,1)} %copy-done.12) | copy-start | bytes 1572868
  244.4 6.4 %collective-permute-start.3 = (bf16[1024,128]{1,0:T(8,128)(2,1)S(1)}, bf16[1024,128]{1,0:T(8,128)(2,1)S(1)}, u32[]{:S(2)}, u32[]{:S(2)}) collective-permute-start(bf16[1024,128]{1,0:T(8,128)(2,1)S(1)} %collective-permute-done.2), channel_id=1, source_target_pairs={{0,32},{4,36},{8,40},{12,44},{16,48},{20,52},{24,56},{28,60},{32,6... | collective-permute-start | bytes 786440 | tf_op jit(solution)/shard_map/ppermute | solution.py:13
  244.4 17.5 %collective-permute-start.10 = (bf16[128,2048]{1,0:T(8,128)(2,1)S(1)}, bf16[128,2048]{1,0:T(8,128)(2,1)S(1)}, u32[]{:S(2)}, u32[]{:S(2)}) collective-permute-start(bf16[128,2048]{1,0:T(8,128)(2,1)S(1)} %collective-permute-done.9), channel_id=1, source_target_pairs={{0,32},{4,36},{8,40},{12,44},{16,48},{20,52},{24,56},{28,60},{32,6... | collective-permute-start | bytes 1572872 | tf_op jit(solution)/shard_map/ppermute | solution.py:13
  250.8 16.7 %collective-permute-start.4 = (bf16[1024,128]{1,0:T(8,128)(2,1)S(1)}, bf16[1024,128]{1,0:T(8,128)(2,1)S(1)}, u32[]{:S(2)}, u32[]{:S(2)}) collective-permute-start(bf16[1024,128]{1,0:T(8,128)(2,1)S(1)} %collective-permute-done.3), channel_id=1, source_target_pairs={{0,32},{4,36},{8,40},{12,44},{16,48},{20,52},{24,56},{28,60},{32,6... | collective-permute-start | bytes 786440 | tf_op jit(solution)/shard_map/ppermute | solution.py:13
  261.9 16.9 %collective-permute-start.11 = (bf16[128,2048]{1,0:T(8,128)(2,1)S(1)}, bf16[128,2048]{1,0:T(8,128)(2,1)S(1)}, u32[]{:S(2)}, u32[]{:S(2)}) collective-permute-start(bf16[128,2048]{1,0:T(8,128)(2,1)S(1)} %collective-permute-done.10), channel_id=1, source_target_pairs={{0,32},{4,36},{8,40},{12,44},{16,48},{20,52},{24,56},{28,60},{32,6... | collective-permute-start | bytes 1572872 | tf_op jit(solution)/shard_map/ppermute | solution.py:13
  267.6 16.9 %collective-permute-start.5 = (bf16[1024,128]{1,0:T(8,128)(2,1)S(1)}, bf16[1024,128]{1,0:T(8,128)(2,1)S(1)}, u32[]{:S(2)}, u32[]{:S(2)}) collective-permute-start(bf16[1024,128]{1,0:T(8,128)(2,1)S(1)} %collective-permute-done.4), channel_id=1, source_target_pairs={{0,32},{4,36},{8,40},{12,44},{16,48},{20,52},{24,56},{28,60},{32,6... | collective-permute-start | bytes 786440 | tf_op jit(solution)/shard_map/ppermute | solution.py:13
  278.8 23.2 %collective-permute-start.12 = (bf16[128,2048]{1,0:T(8,128)(2,1)S(1)}, bf16[128,2048]{1,0:T(8,128)(2,1)S(1)}, u32[]{:S(2)}, u32[]{:S(2)}) collective-permute-start(bf16[128,2048]{1,0:T(8,128)(2,1)S(1)} %collective-permute-done.11), channel_id=1, source_target_pairs={{0,32},{4,36},{8,40},{12,44},{16,48},{20,52},{24,56},{28,60},{32,6... | collective-permute-start | bytes 1572872 | tf_op jit(solution)/shard_map/ppermute | solution.py:13
  284.4 16.9 %collective-permute-start.6 = (bf16[1024,128]{1,0:T(8,128)(2,1)S(1)}, bf16[1024,128]{1,0:T(8,128)(2,1)S(1)}, u32[]{:S(2)}, u32[]{:S(2)}) collective-permute-start(bf16[1024,128]{1,0:T(8,128)(2,1)S(1)} %collective-permute-done.5), channel_id=1, source_target_pairs={{0,32},{4,36},{8,40},{12,44},{16,48},{20,52},{24,56},{28,60},{32,6... | collective-permute-start | bytes 786440 | tf_op jit(solution)/shard_map/ppermute | solution.py:13
  302.0 11.2 %collective-permute-start.13 = (bf16[128,2048]{1,0:T(8,128)(2,1)S(1)}, bf16[128,2048]{1,0:T(8,128)(2,1)S(1)}, u32[]{:S(2)}, u32[]{:S(2)}) collective-permute-start(bf16[128,2048]{1,0:T(8,128)(2,1)S(1)} %collective-permute-done.12), channel_id=1, source_target_pairs={{0,32},{4,36},{8,40},{12,44},{16,48},{20,52},{24,56},{28,60},{32,6... | collective-permute-start | bytes 1572872 | tf_op jit(solution)/shard_map/ppermute | solution.py:13
  318.8 5.4 copy-start.3
  329.7 2.0 copy-start.7
  329.7 2.0 copy-start.9
  331.7 21.6 %collective-permute-start.21 = (f32[128,2048]{1,0:T(8,128)}, f32[128,2048]{1,0:T(8,128)}, u32[]{:S(2)}, u32[]{:S(2)}) collective-permute-start(f32[128,2048]{1,0:T(8,128)} %fusion.24), channel_id=1, source_target_pairs={{0,32},{4,36},{8,40},{12,44},{16,48},{20,52},{24,56},{28,60},{32,6... | collective-permute-start | bytes 3145736 | tf_op jit(solution)/shard_map/ppermute | solution.py:13
  336.8 18.6 %copy-start.8 = (bf16[768,1024]{1,0:T(8,128)(2,1)S(1)}, bf16[768,1024]{1,0:T(8,128)(2,1)}, u32[]{:S(2)}) copy-start(bf16[768,1024]{1,0:T(8,128)(2,1)} %copy-done.7) | copy-start | bytes 4718596
  355.3 20.6 %collective-permute-start.22 = (f32[128,2048]{1,0:T(8,128)S(1)}, f32[128,2048]{1,0:T(8,128)S(1)}, u32[]{:S(2)}, u32[]{:S(2)}) collective-permute-start(f32[128,2048]{1,0:T(8,128)S(1)} %convolution_add_fusion), channel_id=1, source_target_pairs={{0,32},{4,36},{8,40},{12,44},{16,48},{20,52},{24,56},{28,60},{32,6... | collective-permute-start | bytes 3145736 | tf_op jit(solution)/shard_map/ppermute | solution.py:13
  356.0 20.1 %copy-start.4 = (bf16[768,1024]{1,0:T(8,128)(2,1)S(1)}, bf16[768,1024]{1,0:T(8,128)(2,1)}, u32[]{:S(2)}) copy-start(bf16[768,1024]{1,0:T(8,128)(2,1)} %all_to_all.23) | copy-start | bytes 4718596
  356.0 20.1 %copy-start.10 = (bf16[768,1024]{1,0:T(8,128)(2,1)S(1)}, bf16[768,1024]{1,0:T(8,128)(2,1)}, u32[]{:S(2)}) copy-start(bf16[768,1024]{1,0:T(8,128)(2,1)} %copy-done.9) | copy-start | bytes 4718596
  376.0 21.5 %collective-permute-start.23 = (f32[128,2048]{1,0:T(8,128)S(1)}, f32[128,2048]{1,0:T(8,128)S(1)}, u32[]{:S(2)}, u32[]{:S(2)}) collective-permute-start(f32[128,2048]{1,0:T(8,128)S(1)} %add.244), channel_id=1, source_target_pairs={{0,32},{4,36},{8,40},{12,44},{16,48},{20,52},{24,56},{28,60},{32,6... | collective-permute-start | bytes 3145736 | tf_op jit(solution)/shard_map/ppermute | solution.py:13
  376.5 32.2 %collective-permute-start.14 = (f32[128,1024]{1,0:T(8,128)S(1)}, f32[128,1024]{1,0:T(8,128)S(1)}, u32[]{:S(2)}, u32[]{:S(2)}) collective-permute-start(f32[128,1024]{1,0:T(8,128)S(1)} %fusion.39), channel_id=1, source_target_pairs={{0,32},{4,36},{8,40},{12,44},{16,48},{20,52},{24,56},{28,60},{32,6... | collective-permute-start | bytes 1572872 | tf_op jit(solution)/shard_map/ppermute | solution.py:13
  397.6 33.6 %collective-permute-start.24 = (f32[128,2048]{1,0:T(8,128)S(1)}, f32[128,2048]{1,0:T(8,128)S(1)}, u32[]{:S(2)}, u32[]{:S(2)}) collective-permute-start(f32[128,2048]{1,0:T(8,128)S(1)} %add.245), channel_id=1, source_target_pairs={{0,32},{4,36},{8,40},{12,44},{16,48},{20,52},{24,56},{28,60},{32,6... | collective-permute-start | bytes 3145736 | tf_op jit(solution)/shard_map/ppermute | solution.py:13
  409.1 33.3 %collective-permute-start.15 = (f32[128,1024]{1,0:T(8,128)S(1)}, f32[128,1024]{1,0:T(8,128)S(1)}, u32[]{:S(2)}, u32[]{:S(2)}) collective-permute-start(f32[128,1024]{1,0:T(8,128)S(1)} %convolution_add_fusion.1), channel_id=1, source_target_pairs={{0,32},{4,36},{8,40},{12,44},{16,48},{20,52},{24,56},{28,60},{32,6... | collective-permute-start | bytes 1572872 | tf_op jit(solution)/shard_map/ppermute | solution.py:13
  431.3 45.6 %collective-permute-start.25 = (f32[128,2048]{1,0:T(8,128)S(1)}, f32[128,2048]{1,0:T(8,128)S(1)}, u32[]{:S(2)}, u32[]{:S(2)}) collective-permute-start(f32[128,2048]{1,0:T(8,128)S(1)} %add.246), channel_id=1, source_target_pairs={{0,32},{4,36},{8,40},{12,44},{16,48},{20,52},{24,56},{28,60},{32,6... | collective-permute-start | bytes 3145736 | tf_op jit(solution)/shard_map/ppermute | solution.py:13
  442.5 33.6 %collective-permute-start.16 = (f32[128,1024]{1,0:T(8,128)S(1)}, f32[128,1024]{1,0:T(8,128)S(1)}, u32[]{:S(2)}, u32[]{:S(2)}) collective-permute-start(f32[128,1024]{1,0:T(8,128)S(1)} %add.235), channel_id=1, source_target_pairs={{0,32},{4,36},{8,40},{12,44},{16,48},{20,52},{24,56},{28,60},{32,6... | collective-permute-start | bytes 1572872 | tf_op jit(solution)/shard_map/ppermute | solution.py:13
  476.2 12.0 %collective-permute-start.17 = (f32[128,1024]{1,0:T(8,128)S(1)}, f32[128,1024]{1,0:T(8,128)S(1)}, u32[]{:S(2)}, u32[]{:S(2)}) collective-permute-start(f32[128,1024]{1,0:T(8,128)S(1)} %add.236), channel_id=1, source_target_pairs={{0,32},{4,36},{8,40},{12,44},{16,48},{20,52},{24,56},{28,60},{32,6... | collective-permute-start | bytes 1572872 | tf_op jit(solution)/shard_map/ppermute | solution.py:13
  478.0 45.1 %collective-permute-start.26 = (f32[128,2048]{1,0:T(8,128)}, f32[128,2048]{1,0:T(8,128)}, u32[]{:S(2)}, u32[]{:S(2)}) collective-permute-start(f32[128,2048]{1,0:T(8,128)} %add.247), channel_id=1, source_target_pairs={{0,32},{4,36},{8,40},{12,44},{16,48},{20,52},{24,56},{28,60},{32,6... | collective-permute-start | bytes 3145736 | tf_op jit(solution)/shard_map/ppermute | solution.py:13
  489.0 31.3 %collective-permute-start.18 = (f32[128,1024]{1,0:T(8,128)}, f32[128,1024]{1,0:T(8,128)}, u32[]{:S(2)}, u32[]{:S(2)}) collective-permute-start(f32[128,1024]{1,0:T(8,128)} %add.237), channel_id=1, source_target_pairs={{0,32},{4,36},{8,40},{12,44},{16,48},{20,52},{24,56},{28,60},{32,6... | collective-permute-start | bytes 1572872 | tf_op jit(solution)/shard_map/ppermute | solution.py:13
  521.4 11.7 %collective-permute-start.19 = (f32[128,1024]{1,0:T(8,128)S(1)}, f32[128,1024]{1,0:T(8,128)S(1)}, u32[]{:S(2)}, u32[]{:S(2)}) collective-permute-start(f32[128,1024]{1,0:T(8,128)S(1)} %add.238), channel_id=1, source_target_pairs={{0,32},{4,36},{8,40},{12,44},{16,48},{20,52},{24,56},{28,60},{32,6... | collective-permute-start | bytes 1572872 | tf_op jit(solution)/shard_map/ppermute | solution.py:13
  523.1 2.5 copy-start.5
  525.5 65.1 %collective-permute-start.27 = (f32[128,2048]{1,0:T(8,128)}, f32[128,2048]{1,0:T(8,128)}, u32[]{:S(2)}, u32[]{:S(2)}) collective-permute-start(f32[128,2048]{1,0:T(8,128)} %add.248), channel_id=1, source_target_pairs={{0,32},{4,36},{8,40},{12,44},{16,48},{20,52},{24,56},{28,60},{32,6... | collective-permute-start | bytes 3145736 | tf_op jit(solution)/shard_map/ppermute | solution.py:13
  534.0 31.3 %collective-permute-start.20 = (f32[128,1024]{1,0:T(8,128)}, f32[128,1024]{1,0:T(8,128)}, u32[]{:S(2)}, u32[]{:S(2)}) collective-permute-start(f32[128,1024]{1,0:T(8,128)} %add.239), channel_id=1, source_target_pairs={{0,32},{4,36},{8,40},{12,44},{16,48},{20,52},{24,56},{28,60},{32,6... | collective-permute-start | bytes 1572872 | tf_op jit(solution)/shard_map/ppermute | solution.py:13
  538.0 48.1 %all-to-all-start.2 = ((bf16[256,64,12]{0,2,1:T(8,128)(2,1)}), bf16[256,64,12]{0,2,1:T(8,128)(2,1)}, u32[]{:S(2)}, u32[]{:S(2)}) async-start(bf16[256,64,12]{0,2,1:T(8,128)(2,1)} %all_to_all.24), calls=%async_computation.3 | async-start | bytes 1048576 | tf_op jit(solution)/shard_map/all_to_all | solution.py:84
  567.2 23.4 %copy-start.6 = (f32[128,2048]{1,0:T(8,128)S(1)}, f32[128,2048]{1,0:T(8,128)}, u32[]{:S(2)}) copy-start(f32[128,2048]{1,0:T(8,128)} %fusion.11) | copy-start | bytes 3145732
  587.2 5.5 copy-start.1
Sparse Core Ops, SparseCore 0:
  336.9 44.0 reduce-scatter.1
where the time goes:
time: 610 us; the launch traced here: 600 us
  waiting for transfers between devices  424 us (70%)
  local copies, waits for them, and re-layouts  58.1 us (10%)
  starting transfers between devices  46.3 us (8%)
  matrix products  33.7 us (6%)
  other arithmetic  23 us (4%)
  between operations  15.2 us (2%)
    ppermute x28, waiting for transfers between devices, shifted(): lax.ppermute(value, axis, [(i, (i + by) % peers) for i in range(peers)])  372 us
    all_to_all x1, waiting for transfers between devices, shards(): lax.all_to_all(packed_x, 'ep', split_axis=0, concat_axis=0, tiled=True)  32.9 us
    all_to_all x1, starting transfers between devices, shards(): lax.all_to_all(summed.astype(jnp.bfloat16), 'ep', split_axis=1, concat_ax...  22.8 us
    all_to_all x1, waiting for transfers between devices, shards(): lax.all_to_all(summed.astype(jnp.bfloat16), 'ep', split_axis=1, concat_ax...  18.8 us
    all_to_all x1, starting transfers between devices, shards(): lax.all_to_all(packed_x, 'ep', split_axis=0, concat_axis=0, tiled=True)  13 us
  transfers between devices with their start and end apart: 32, of which 23 were waited for; matrix products, arithmetic and copies ran while one was open for 12% of the time, Pallas kernels for 0%

commit v1 on v0

v1 whole, which is shorter than its diff:
```python
import functools
import math

import jax
import jax.numpy as jnp
from jax import lax
from jax.experimental import pallas as pl
from jax.experimental.pallas import tpu as pltpu
from jax.sharding import PartitionSpec as P

MESH = pl.DeviceIdType.MESH
E = 8
NZ, NX, NC, NY = 8, 4, 2, 4
SLOTS = 96
ROWS = E * SLOTS
TOK = 256
DIN = 1024
DOUT = 2048
SPAN = 128
QY = DOUT // NY
QX = DIN // NY
TILE = 256
NT = ROWS // TILE
F32 = jnp.float32
BF16 = jnp.bfloat16


def dot_nn(a, b):
    return lax.dot_general(a, b, (((1,), (0,)), ((), ())), preferred_element_type=F32)


def dot_nt(a, b):
    return lax.dot_general(a, b, (((1,), (1,)), ((), ())), preferred_element_type=F32)


def dot_tn(a, b):
    return lax.dot_general(a, b, (((0,), (0,)), ((), ())), preferred_element_type=F32)


def gelu_parts(v):
    k = math.sqrt(2.0 / math.pi)
    vv = v * v
    t = jnp.tanh(k * (v + 0.044715 * (v * vv)))
    half = 0.5 * (1.0 + t)
    act = v * half
    slope = half + 0.5 * v * (1.0 - t * t) * (k * (1.0 + 3.0 * 0.044715 * vv))
    return act, slope


def kernel(
    grad_scale,
    x_ref, dy_ref, ids_ref, gate_ref, w1_ref, w2_ref,
    gin_ref, g1_ref, g2_ref,
    p_ref, pg_ref, packx, packy, xr, dyr, w1b, w2b, actt, bpret,
    own, sbuf, rbuf, partown, parts, partr, retb, retr,
    ag_s, ag_r, rs_s, rs_r, dx_s, dx_r, dc_s, dc_r, fw_s, fw_r, pt_s, pt_r, rt_s, rt_r,
):
    ep = lax.axis_index("ep")
    y = lax.axis_index("tp")
    z = ep // E
    me = lax.rem(ep, E)
    x = me // NC
    c = lax.rem(me, NC)
    right = (lax.rem(z + 1, NZ) * E + me, y)
    left = (lax.rem(z + NZ - 1, NZ) * E + me, y)

    def plane(e):
        return (z * E + e, y)

    def yrank(k):
        return lax.rem(y + k, NY)

    def remote(src, dst, ss, rs, dev):
        return pltpu.make_async_remote_copy(
            src_ref=src, dst_ref=dst, send_sem=ss, recv_sem=rs, device_id=dev, device_id_type=MESH
        )

    bar = pltpu.get_barrier_semaphore()
    for dev in (left, right):
        pl.semaphore_signal(bar, inc=1, device_id=dev, device_id_type=MESH)
    for k in range(1, E):
        pl.semaphore_signal(bar, inc=1, device_id=plane(lax.rem(me + k, E)), device_id_type=MESH)
    for k in range(1, NY):
        pl.semaphore_signal(bar, inc=1, device_id=(ep, yrank(k)), device_id_type=MESH)
    pl.semaphore_wait(bar, 2 + E - 1 + NY - 1)

    def wchunk(slot, ch):
        return w1b.at[slot] if ch == 0 else w2b.at[slot, ch - 1]

    def ag(direction, step, ch):
        if step == 0:
            src_slot = 0
        else:
            src_slot = 2 * step - 1 + direction
        dst_slot = 7 if step == 3 else 2 * step + 1 + direction
        src, dst = wchunk(src_slot, ch), wchunk(dst_slot, ch)
        if step == 3:
            half = pl.ds(direction * (SPAN // 2), SPAN // 2)
            src, dst = src.at[half], dst.at[half]
        return remote(src, dst, ag_s.at[direction, step, ch], ag_r.at[direction, step, ch],
                      left if direction == 0 else right)

    order = (1, 2, 0)
    for h in range(2):
        w2b[0, h] = w2_ref[0, :, h * DIN:(h + 1) * DIN]
        for direction in range(2):
            ag(direction, 0, 1 + h).start()
    w1b[0] = w1_ref[0].astype(F32).T.astype(BF16)
    for direction in range(2):
        ag(direction, 0, 0).start()

    def ag_pass(step):
        for ch in order:
            for direction in range(2):
                ag(direction, step - 1, ch).wait_recv()
                if step <= 3:
                    ag(direction, step, ch).start()

    lanes = lax.broadcasted_iota(jnp.int32, (TOK, 128), 1)
    first = ids_ref[:, 0:1] == lanes
    second = ids_ref[:, 1:2] == lanes
    named = jnp.where(first | second, 1.0, 0.0)
    gates = gate_ref[...].astype(F32) * (1.0 / 16.0)
    gate_of = jnp.where(first, gates[:, 0:1], 0.0) + jnp.where(second, gates[:, 1:2], 0.0)
    named_t = named.T[:16]
    gate_t = gate_of.T[:16].astype(BF16)
    before = (
        lax.broadcasted_iota(jnp.int32, (TOK, TOK), 0) < lax.broadcasted_iota(jnp.int32, (TOK, TOK), 1)
    ).astype(F32).astype(BF16)
    rank = dot_nn(named_t.astype(BF16), before)
    rank = jnp.where(named_t > 0.5, rank, -1.0).astype(BF16)
    for e in range(E):
        slot = lax.broadcasted_iota(jnp.int32, (SLOTS, TOK), 0).astype(F32)
        hit = jnp.broadcast_to(rank[e:e + 1].astype(F32), (SLOTS, TOK)) == slot
        p_ref[e * SLOTS:(e + 1) * SLOTS] = jnp.where(hit, 1.0, 0.0).astype(BF16)
        pg_ref[e * SLOTS:(e + 1) * SLOTS] = jnp.where(
            hit, jnp.broadcast_to(gate_t[e:e + 1].astype(F32), (SLOTS, TOK)), 0.0
        ).astype(BF16)

    def rows_of(e):
        return pl.ds(pl.multiple_of(e * SLOTS, 32), SLOTS)

    mine = rows_of(me)
    sib = me + 1 - 2 * c

    def cot_send(e):
        return remote(packy.at[y, rows_of(e)], dyr.at[y, mine], dc_s.at[e], dc_r.at[me], plane(e))

    def cot_recv(e):
        return remote(packy.at[y, rows_of(e)], dyr.at[y, rows_of(e)], dc_s.at[e], dc_r.at[e], plane(e))

    def cot_sib(target, source):
        return remote(packy.at[:, rows_of(target)], dyr.at[:, rows_of(source)], dc_s.at[target], dc_r.at[source],
                      plane(target))

    def pack_cot(e):
        rows = rows_of(e)
        for q in range(NY):
            packy[q, rows] = dot_nn(pg_ref[rows], dy_ref[:, q * QY:(q + 1) * QY]).astype(BF16)

    far = E - NC

    def other(k):
        return lax.rem(x * NC + NC + k, E)

    @pl.loop(0, far)
    def _(k):
        e = other(k)
        pack_cot(e)
        cot_send(e).start()

    def feat_send(e):
        return remote(packx.at[rows_of(e)], xr.at[mine], dx_s.at[e], dx_r.at[me], plane(e))

    def feat_recv(e):
        return remote(packx.at[rows_of(e)], xr.at[rows_of(e)], dx_s.at[e], dx_r.at[e], plane(e))

    def pack_feat(e):
        rows = rows_of(e)
        packx[rows] = dot_nn(p_ref[rows], x_ref[...]).astype(BF16)

    @pl.loop(0, far)
    def _(k):
        e = other(k)
        pack_feat(e)
        feat_send(e).start()

    pack_cot(sib)
    cot_sib(sib, me).start()
    pack_feat(sib)
    feat_send(sib).start()
    for q in range(NY):
        dyr[q, mine] = dot_nn(pg_ref[mine], dy_ref[:, q * QY:(q + 1) * QY]).astype(BF16)
    xr[mine] = dot_nn(p_ref[mine], x_ref[...]).astype(BF16)

    def chip_rows(k):
        return pl.ds(pl.multiple_of(lax.rem(x + k, NX) * NC * SLOTS, 64), NC * SLOTS)

    def fw_send(k, j):
        part = dyr.at[y, chip_rows(k)]
        return remote(part, part, fw_s.at[k - 1, j - 1], fw_r.at[k - 1, j - 1], (ep, yrank(j)))

    def fw_recv(k, j):
        part = dyr.at[yrank(NY - j), chip_rows(k)]
        return remote(part, part, fw_s.at[k - 1, j - 1], fw_r.at[k - 1, j - 1], (ep, yrank(j)))

    for k in (1, 3, 2):
        for cc in range(NC):
            cot_recv(lax.rem(x + k, NX) * NC + cc).wait_recv()
        for j in (1, 3, 2):
            fw_send(k, j).start()

    ag_pass(1)

    def forward(s0, n):
        w1 = w1b[s0:s0 + n].reshape(n * SPAN, DIN)
        w2 = [w2b[s0:s0 + n, h].reshape(n * SPAN, DIN) for h in range(2)]

        @pl.loop(0, NT)
        def _(t):
            rows = pl.ds(pl.multiple_of(t * TILE, TILE), TILE)
            pre = dot_nt(w1, xr[rows])
            back = dot_nt(w2[0][:, :QY], dyr[0, rows])
            for q in range(1, NY):
                back += dot_nt(w2[q // 2][:, (q % 2) * QY:(q % 2 + 1) * QY], dyr[q, rows])
            act, slope = gelu_parts(pre)
            actt[t, s0:s0 + n] = act.astype(BF16).reshape(n, SPAN, TILE)
            bpret[t, s0:s0 + n] = (back * slope).astype(BF16).reshape(n, SPAN, TILE)

    def weight_grads(s0, n):
        def lhs(buf, t):
            return buf[t, s0:s0 + n].reshape(n * SPAN, TILE)

        for half in range(2):
            cols = slice(half * 512, (half + 1) * 512)
            total = dot_nn(lhs(bpret, 0), xr[0:TILE, cols])
            for t in range(1, NT):
                total += dot_nn(lhs(bpret, t), xr[t * TILE:(t + 1) * TILE, cols])
            own[0:n, 0, :, cols] = total.reshape(n, SPAN, 512)
        for q in range(NY):
            total = dot_nn(lhs(actt, 0), dyr[q, 0:TILE])
            for t in range(1, NT):
                total += dot_nn(lhs(actt, t), dyr[q, t * TILE:(t + 1) * TILE])
            own[0:n, 1 + q // 2, :, (q % 2) * QY:(q % 2 + 1) * QY] = total.reshape(n, SPAN, QY)

    @pl.loop(1, E)
    def _(k):
        feat_recv(lax.rem(me + k, E)).wait_recv()

    ag_pass(2)
    cot_sib(sib, sib).wait_recv()
    for k in (1, 3, 2):
        for j in (1, 3, 2):
            fw_recv(k, j).wait_recv()
    forward(0, 1)
    forward(1, 2)
    forward(3, 2)
    ag_pass(3)
    forward(5, 2)

    def rs(direction, step, ch):
        src, dst = sbuf.at[direction, step, ch], rbuf.at[direction, step, ch]
        if step == 0:
            half = pl.ds(direction * (SPAN // 2), SPAN // 2)
            src, dst = src.at[half], dst.at[half]
        return remote(src, dst, rs_s.at[direction, step, ch], rs_r.at[direction, step, ch],
                      right if direction == 0 else left)

    ag_pass(4)
    forward(7, 1)
    weight_grads(7, 1)
    for ch in order:
        for direction in range(2):
            half = slice(direction * (SPAN // 2), (direction + 1) * (SPAN // 2))
            sbuf[direction, 0, ch, half] = own[0, ch, half].astype(BF16)
            rs(direction, 0, ch).start()

    def rs_pass(step):
        for ch in order:
            for direction in range(2):
                rs(direction, step - 1, ch).wait_recv()
                if step == 1:
                    got = slice(direction * (SPAN // 2), (direction + 1) * (SPAN // 2))
                    rest = slice((1 - direction) * (SPAN // 2), (2 - direction) * (SPAN // 2))
                    sbuf[direction, step, ch, rest] = own[direction, ch, rest].astype(BF16)
                else:
                    got = slice(0, SPAN)
                sbuf[direction, step, ch, got] = (
                    own[direction, ch, got] + rbuf[direction, step - 1, ch, got].astype(F32)
                ).astype(BF16)
                rs(direction, step, ch).start()

    weight_grads(5, 2)
    rs_pass(1)
    weight_grads(3, 2)

    def part_send(j):
        return remote(parts.at[j - 1], partr.at[j - 1], pt_s.at[j - 1], pt_r.at[j - 1], (ep, yrank(j)))

    def part_dot(t, q):
        cols = pl.ds(pl.multiple_of(q * QX, QX), QX)
        return dot_tn(bpret[t].reshape(NZ * SPAN, TILE), w1b[:, :, cols].reshape(NZ * SPAN, QX))

    for j in (2, 1, 3):
        @pl.loop(0, NT)
        def _(t):
            rows = pl.ds(pl.multiple_of(t * TILE, TILE), TILE)
            parts[j - 1, rows] = part_dot(t, yrank(j)).astype(BF16)
        part_send(j).start()

    @pl.loop(0, NT)
    def _(t):
        partown[pl.ds(pl.multiple_of(t * TILE, TILE), TILE)] = part_dot(t, y)

    rs_pass(2)
    weight_grads(1, 2)

    def ret_send(e):
        return remote(retb.at[rows_of(e)], retr.at[mine], rt_s.at[e], rt_r.at[me], plane(e))

    def ret_recv(e):
        return remote(retb.at[rows_of(e)], retr.at[rows_of(e)], rt_s.at[e], rt_r.at[e], plane(e))

    for j in (1, 3, 2):
        part_send(j).wait_recv()
    retb[...] = (
        partown[...] + partr[0].astype(F32) + partr[1].astype(F32) + partr[2].astype(F32)
    ).astype(BF16)

    @pl.loop(1, E)
    def _(k):
        ret_send(lax.rem(me + k, E)).start()

    retr[mine] = retb[mine]
    rs_pass(3)
    weight_grads(0, 1)

    @pl.loop(1, E)
    def _(k):
        ret_recv(lax.rem(me + k, E)).wait_recv()

    gin_ref[...] = dot_tn(p_ref[...], retr[...]).astype(BF16)

    for ch in order:
        for direction in range(2):
            rs(direction, 3, ch).wait_recv()
        total = (own[0, ch] + rbuf[0, 3, ch].astype(F32) + rbuf[1, 3, ch].astype(F32)) * grad_scale
        if ch == 0:
            g1_ref[0] = total.T.astype(BF16)
        else:
            g2_ref[0, :, (ch - 1) * DIN:ch * DIN] = total.astype(BF16)

    for step in range(4):
        for ch in order:
            for direction in range(2):
                ag(direction, step, ch).wait_send()
                rs(direction, step, ch).wait_send()

    @pl.loop(0, far)
    def _(k):
        cot_send(other(k)).wait_send()

    cot_sib(sib, me).wait_send()
    for k in range(1, NX):
        for j in range(1, NY):
            fw_send(k, j).wait_send()
    for j in range(1, NY):
        part_send(j).wait_send()

    @pl.loop(1, E)
    def _(k):
        feat_send(lax.rem(me + k, E)).wait_send()
        ret_send(lax.rem(me + k, E)).wait_send()


def shards(features, cotangent, expert_ids, gate_levels, w_in, w_out):
    tokens = features.shape[0] * lax.axis_size("ep")
    grad_scale = 1.0 / math.sqrt(2.0 * tokens / E)
    vm = pl.BlockSpec(memory_space=pltpu.VMEM)
    dma = pltpu.SemaphoreType.DMA


    return pl.pallas_call(
        functools.partial(kernel, grad_scale),
        out_shape=(
            jax.ShapeDtypeStruct((TOK, QX), BF16),
            jax.ShapeDtypeStruct((1, DIN, SPAN), BF16),
            jax.ShapeDtypeStruct((1, SPAN, DOUT), BF16),
        ),
        in_specs=[vm] * 6,
        out_specs=(vm, vm, vm),
        scratch_shapes=[
            pltpu.VMEM((ROWS, TOK), BF16),
            pltpu.VMEM((ROWS, TOK), BF16),
            pltpu.VMEM((ROWS, DIN), BF16),
            pltpu.VMEM((NY, ROWS, QY), BF16),
            pltpu.VMEM((ROWS, DIN), BF16),
            pltpu.VMEM((NY, ROWS, QY), BF16),
            pltpu.VMEM((NZ, SPAN, DIN), BF16),
            pltpu.VMEM((NZ, 2, SPAN, DIN), BF16),
            pltpu.VMEM((NT, NZ, SPAN, TILE), BF16),
            pltpu.VMEM((NT, NZ, SPAN, TILE), BF16),
            pltpu.VMEM((2, 3, SPAN, DIN), F32),
            pltpu.VMEM((2, 4, 3, SPAN, DIN), BF16),
            pltpu.VMEM((2, 4, 3, SPAN, DIN), BF16),
            pltpu.VMEM((ROWS, QX), F32),
            pltpu.VMEM((NY - 1, ROWS, QX), BF16),
            pltpu.VMEM((NY - 1, ROWS, QX), BF16),
            pltpu.VMEM((ROWS, QX), BF16),
            pltpu.VMEM((ROWS, QX), BF16),
            dma((2, 4, 3)), dma((2, 4, 3)),
            dma((2, 4, 3)), dma((2, 4, 3)),
            dma((E,)), dma((E,)),
            dma((E,)), dma((E,)),
            dma((NX - 1, NY - 1)), dma((NX - 1, NY - 1)),
            dma((NY - 1,)), dma((NY - 1,)),
            dma((E,)), dma((E,)),
        ],
        compiler_params=pltpu.CompilerParams(
            collective_id=0, has_side_effects=True, vmem_limit_bytes=60 * 1024 * 1024
        ),
        cost_estimate=pl.CostEstimate(flops=11_300_000_000, bytes_accessed=5_000_000, transcendentals=0),
        name="moe_backward",
    )(features, cotangent, expert_ids, gate_levels, w_in, w_out)


def solution(mesh):
    return jax.shard_map(
        shards,
        mesh=mesh,
        in_specs=(
            P("ep", None),
            P("ep", None),
            P("ep", None),
            P("ep", None),
            P("ep", None, "tp"),
            P("ep", "tp", None),
        ),
        out_specs=(P("ep", "tp"), P("ep", None, "tp"), P("ep", "tp", None)),
        check_vma=False,
    )
```

time: 610 us -> 144 us (0.24); the launches traced: 600 us -> 143 us
  waiting for transfers between devices: 424 us -> 0 us
  Pallas kernels: 0 us -> 136 us
  local copies, waits for them, and re-layouts: 58.1 us -> 6.38 us
  starting transfers between devices: 46.3 us -> 0 us
  matrix products: 33.7 us -> 0 us
  other arithmetic: 23 us -> 0 us
  between operations: 15.2 us -> 0.66 us
    ppermute x28 -> x0, waiting for transfers between devices: 372 us -> none  [shifted(): lax.ppermute(value, axis, [(i, (i + by) % peers) for i in range(peers)])]
    pallas_call x0 -> x1, Pallas kernels: none -> 136 us  [shards(): pl.pallas_call(functools.partial(kernel, grad_scale), out_shape=(jax.Shap...]
    all_to_all x3 -> x0, waiting for transfers between devices: 51.8 us -> none  [the longest x1 32.9 us: shards(): lax.all_to_all(packed_x, 'ep', split_axis=0, concat_axis=0, tiled=True)]
    all_to_all x3 -> x0, starting transfers between devices: 43 us -> none  [the longest x1 22.8 us: shards(): lax.all_to_all(summed.astype(jnp.bfloat16), 'ep', split_axis=1, concat_ax...]
    dot_general x19 -> x0, matrix products: 33.7 us -> none  [the longest x8 10.5 us: span_grads(): lax.dot_general(act_cols, rows_dy, (((0,), (0,)), ((), ())), preferred_el...]
    gather x5 -> x0, local copies, waits for them, and re-layouts: 17.1 us -> none  [the longest x2 5.91 us: shards(): packed_x = features[token_ids] * slot_mask]
    dynamic_update_slice x16 -> x0, local copies, waits for them, and re-layouts: 15.7 us -> none  [the longest x7 7.07 us: shards(): lax.dynamic_update_slice_in_dim(weight_in, moving[0], anchor * span, 1)]
    all_to_all x4 -> x0, local copies, waits for them, and re-layouts: 8.05 us -> none  [the longest x1 4.72 us: shards(): lax.all_to_all(packed_dy, 'ep', split_axis=0, concat_axis=0, tiled=True)]
  transfers between devices with their start and end apart: 32 -> 0, of which waited for: 23 -> 0; matrix products, arithmetic and copies ran while one was open for 12% -> 0% of each run, Pallas kernels for 0% -> 0%
where the time goes in v1:
time: 144 us; the launch traced here: 143 us
  Pallas kernels  136 us (94%)
  local copies, waits for them, and re-layouts  6.38 us (4%)
    pallas_call x1, Pallas kernels, shards(): pl.pallas_call(functools.partial(kernel, grad_scale), out_shape=(jax.Shap...  136 us
    unnamed x9, local copies, waits for them, and re-layouts  6.38 us

profile of v1, /device:TPU:1, one launch (start us, length us, event | category | flops | bytes accessed | tf_op | source)
XLA Modules:
  0.0 143.3 jit_solution(11046718773407365062)
XLA Ops:
  0.6 0.0 copy-start.1
  0.6 1.5 %copy.9.ids_ref = s32[256,2]{1,0:T(8,128)} copy(s32[256,2]{0,1:T(2,128)} %param.8) | data formatting | bytes 4096 | tf_op args[2]
  2.1 0.0 copy-done.1
  2.1 0.8 copy.10.gate_ref
  2.9 136.2 %moe_backward.1 = (bf16[256,256]{1,0:T(8,128)(2,1)}, bf16[1,1024,128]{2,1,0:T(8,128)(2,1)}, bf16[1,128,2048]{2,1,0:T(8,128)(2,1)}) custom-call(bf16[256,1024]{1,0:T(8,128)(2,1)} %x_ref.1, bf16[256,2048]{1,0:T(8,128)(2,1)} %dy_ref.1, s32[256,2]{1,0:T(8,128)} %copy.9.ids_ref, s32[256,2]{1,0:T(8,128)} %copy.10.gate_ref, bf16[1,1024,128]{2,1,0:T(8,128)(2,1)} %w1_ref.1, ...), custom_call_target="tpu_custom_call" | custom-call | flops 11299999744 | bytes 5000000 | tf_op jit(solution)/shard_map/moe_backward/pallas_call | solution.py:383
  139.2 0.0 copy-start
  139.2 1.6 %copy.14 = bf16[256,256]{1,0:T(8,128)(2,1)} copy(bf16[256,256]{1,0:T(8,128)(2,1)} %get-tuple-element.6) | data formatting | bytes 262144
  140.8 1.7 %copy.15 = bf16[1,1024,128]{2,1,0:T(8,128)(2,1)} copy(bf16[1,1024,128]{2,1,0:T(8,128)(2,1)} %get-tuple-element.7) | data formatting | bytes 524288
  142.5 0.0 copy-done
  142.5 0.8 copy.16
Async XLA Ops:
  0.6 1.5 %copy-start.1 = (s32[256,2]{0,1:T(2,128)S(1)}, s32[256,2]{0,1:T(2,128)}, u32[]{:S(2)}) copy-start(s32[256,2]{0,1:T(2,128)} %param.9) | copy-start | bytes 6148
  139.2 3.3 %copy-start = (bf16[1,128,2048]{2,1,0:T(8,128)(2,1)S(1)}, bf16[1,128,2048]{2,1,0:T(8,128)(2,1)}, u32[]{:S(2)}) copy-start(bf16[1,128,2048]{2,1,0:T(8,128)(2,1)} %get-tuple-element.8) | copy-start | bytes 1572868

commit v2 on v0

v2 whole, which is shorter than its diff:
```python
import functools
import math

import jax
import jax.numpy as jnp
from jax import lax
from jax.experimental import pallas as pl
from jax.experimental.pallas import tpu as pltpu
from jax.sharding import PartitionSpec as P

MESH = pl.DeviceIdType.MESH
E = 8
NZ, NX, NC, NY = 8, 4, 2, 4
TOK = 256
QT = TOK // NY
DIN = 1024
DOUT = 2048
SPAN = 128
QX = DIN // NY
SL = 48
G = NX * SL
CB = 512
WB = DIN + CB
WA = DOUT - CB
HALF = 2 * SPAN
ROWS = NZ * G
F32 = jnp.float32
BF16 = jnp.bfloat16


def dot_nn(a, b):
    return lax.dot_general(a, b, (((1,), (0,)), ((), ())), preferred_element_type=F32)


def dot_nt(a, b):
    return lax.dot_general(a, b, (((1,), (1,)), ((), ())), preferred_element_type=F32)


def dot_tn(a, b):
    return lax.dot_general(a, b, (((0,), (0,)), ((), ())), preferred_element_type=F32)


def gelu_parts(v):
    k = math.sqrt(2.0 / math.pi)
    vv = v * v
    t = jnp.tanh(k * (v + 0.044715 * (v * vv)))
    half = 0.5 * (1.0 + t)
    act = v * half
    slope = half + 0.5 * v * (1.0 - t * t) * (k * (1.0 + 3.0 * 0.044715 * vv))
    return act, slope


def kernel(
    grad_scale,
    x_ref, dy_ref, ids_ref, gate_ref, w1_ref, w2_ref,
    gin_ref, g1_ref, g2_ref,
    rawb, rawa, meta, p_ref, pg_ref, packa, packb, rowsa, rowsb,
    w1v, w1b, w2b, actb, bpb, pown, sbuf, rbuf, gown, gsend, grecv,
    retb, retr, sibs, sibr, giny, gout, gv1, gv2,
    ld, st, zb_s, zb_r, zm_s, zm_r, sb_s, sb_r, sm_s, sm_r, sa_s, sa_r,
    xb_s, xb_r, xa_s, xa_r, za_s, za_r, wy_s, wy_r, rs_s, rs_r, gy_s, gy_r,
    rt_s, rt_r, s2_s, s2_r, yo_s, yo_r,
):
    ep = lax.axis_index("ep")
    y = lax.axis_index("tp")
    z = ep // E
    me = lax.rem(ep, E)
    x = me // NC
    c = lax.rem(me, NC)
    right = (lax.rem(z + 1, NZ) * E + me, y)
    left = (lax.rem(z + NZ - 1, NZ) * E + me, y)
    sibling = (z * E + me + 1 - 2 * c, y)

    def xrank(k):
        return lax.rem(x + k, NX)

    def xdev(k):
        return (z * E + xrank(k) * NC + c, y)

    def yrank(k):
        return lax.rem(y + k, NY)

    def remote(src, dst, ss, rs, dev):
        return pltpu.make_async_remote_copy(
            src_ref=src, dst_ref=dst, send_sem=ss, recv_sem=rs, device_id=dev, device_id_type=MESH
        )

    quarter = pl.ds(pl.multiple_of(y * QT, QT), QT)
    loads = [
        pltpu.make_async_copy(x_ref.at[quarter], rawb.at[0, c, :, pl.ds(0, DIN)], ld.at[0]),
        pltpu.make_async_copy(dy_ref.at[quarter, pl.ds(0, CB)], rawb.at[0, c, :, pl.ds(DIN, CB)], ld.at[1]),
        pltpu.make_async_copy(dy_ref.at[quarter, pl.ds(CB, WA)], rawa.at[c], ld.at[2]),
        pltpu.make_async_copy(w2_ref.at[0], w2b.at[0], ld.at[3]),
        pltpu.make_async_copy(w1_ref.at[0], w1v, ld.at[4]),
    ]
    for load in loads:
        load.start()

    bar = pltpu.get_barrier_semaphore()
    partners = [left, right, sibling]
    partners += [xdev(k) for k in range(1, NX)] + [(ep, yrank(k)) for k in range(1, NY)]
    for dev in partners:
        pl.semaphore_signal(bar, inc=1, device_id=dev, device_id_type=MESH)
    pl.semaphore_wait(bar, len(partners))

    def slots(direction, step):
        src = 0 if step == 0 else 2 * step - 1 + direction
        return src, (7 if step == 3 else 2 * step + 1 + direction)

    def toward(direction):
        return left if direction == 0 else right

    def raw_ring(direction, step):
        s, d = slots(direction, step)
        src, dst = rawb.at[s, c], rawb.at[d, c]
        if step == 3:
            half = pl.ds(direction * (QT // 2), QT // 2)
            src, dst = src.at[half], dst.at[half]
        return remote(src, dst, zb_s.at[direction, step], zb_r.at[direction, step], toward(direction))

    def meta_ring(direction, step):
        s, d = slots(direction, step)
        return remote(meta.at[s, c], meta.at[d, c], zm_s.at[direction, step], zm_r.at[direction, step],
                      toward(direction))

    def has_meta(direction, step):
        return step < 3 or direction == 0

    def row_ring(direction, step, h):
        s, d = slots(direction, step)
        half = pl.ds(h * (G // 2), G // 2)
        return remote(rowsa.at[s, half], rowsa.at[d, half], za_s.at[direction, step, h], za_r.at[direction, step, h],
                      toward(direction))

    def row_halves(direction, step):
        return (direction,) if step == 3 else (0, 1)

    def raw_sib(slot, core):
        return remote(rawb.at[slot, core], rawb.at[slot, core], sb_s.at[slot], sb_r.at[slot], sibling)

    def meta_sib(slot, core):
        return remote(meta.at[slot, core], meta.at[slot, core], sm_s.at[slot], sm_r.at[slot], sibling)

    def cot_sib(core):
        return remote(rawa.at[core], rawa.at[core], sa_s.at[0], sa_r.at[0], sibling)

    loads[2].wait()
    cot_sib(c).start()
    loads[0].wait()
    loads[1].wait()
    raw_sib(0, c).start()
    for direction in range(2):
        raw_ring(direction, 0).start()

    expert = lax.broadcasted_iota(jnp.int32, (16, TOK), 0)
    first = jnp.broadcast_to(ids_ref[0:1], (16, TOK)) == expert
    second = jnp.broadcast_to(ids_ref[1:2], (16, TOK)) == expert
    gates = gate_ref[...].astype(F32) * (1.0 / 16.0)
    named = jnp.where(first | second, 1.0, 0.0)
    gate_of = jnp.where(first, jnp.broadcast_to(gates[0:1], (16, TOK)), 0.0) + jnp.where(
        second, jnp.broadcast_to(gates[1:2], (16, TOK)), 0.0)
    token = lax.broadcasted_iota(jnp.int32, (TOK, SPAN), 0)
    place = lax.broadcasted_iota(jnp.int32, (TOK, SPAN), 1)
    taken = (token - place == QT * (y - c)) & (place >= QT * c) & (place < QT * c + QT)
    pick = jnp.where(taken, 1.0, 0.0).astype(BF16)
    named_q = dot_nn(named.astype(BF16), pick)
    gate_q = dot_nn(gate_of.astype(BF16), pick)
    earlier = jnp.where(
        lax.broadcasted_iota(jnp.int32, (SPAN, SPAN), 0) < lax.broadcasted_iota(jnp.int32, (SPAN, SPAN), 1), 1.0, 0.0
    ).astype(BF16)
    rank = dot_nn(named_q.astype(BF16), earlier)
    base = jnp.where(c == 0, 1.0, 1.0 + SL // NC)
    meta[0, c, 0:16] = jnp.where(named_q > 0.5, rank + base, 0.0).astype(BF16)
    meta[0, c, 16:32] = gate_q.astype(BF16)
    meta_sib(0, c).start()
    for direction in range(2):
        meta_ring(direction, 0).start()

    def w2_send(j):
        return remote(w2b.at[0], w2b.at[NY - j], wy_s.at[j - 1, 1], wy_r.at[NY - j - 1, 1], (ep, yrank(j)))

    def w1_send(j):
        return remote(w1b.at[0], w1b.at[NY - j], wy_s.at[j - 1, 0], wy_r.at[NY - j - 1, 0], (ep, yrank(j)))

    def w2_recv(j):
        return remote(w2b.at[0], w2b.at[j], wy_s.at[j - 1, 1], wy_r.at[j - 1, 1], (ep, yrank(j)))

    def w1_recv(j):
        return remote(w1b.at[0], w1b.at[j], wy_s.at[j - 1, 0], wy_r.at[j - 1, 0], (ep, yrank(j)))

    loads[3].wait()
    for j in (2, 1, 3):
        w2_send(j).start()

    def build(slot):
        both = meta[slot, 0].astype(F32) + meta[slot, 1].astype(F32)
        want = lax.broadcasted_iota(jnp.int32, (SL, SPAN), 0).astype(F32) + 1.0
        for k in range(NX):
            row = jnp.where(c == 0, both[2 * k:2 * k + 1], both[2 * k + 1:2 * k + 2])
            gate = jnp.where(c == 0, both[16 + 2 * k:17 + 2 * k], both[17 + 2 * k:18 + 2 * k])
            hit = jnp.broadcast_to(row, (SL, SPAN)) == want
            p_ref[slot, k * SL:(k + 1) * SL] = jnp.where(hit, 1.0, 0.0).astype(BF16)
            pg_ref[slot, k * SL:(k + 1) * SL] = jnp.where(
                hit, jnp.broadcast_to(gate, (SL, SPAN)), 0.0).astype(BF16)

    def xrows(k):
        return pl.ds(pl.multiple_of(k * SL, 16), SL)

    def packb_send(slot, k):
        return remote(packb.at[slot, xrows(xrank(k))], rowsb.at[slot, xrows(x)], xb_s.at[slot, k - 1],
                      xb_r.at[slot, k - 1], xdev(k))

    def packb_recv(slot, k):
        return remote(packb.at[slot, xrows(xrank(k))], rowsb.at[slot, xrows(xrank(NX - k))], xb_s.at[slot, k - 1],
                      xb_r.at[slot, k - 1], xdev(k))

    def packa_send(k):
        return remote(packa.at[xrows(xrank(k))], rowsa.at[0, xrows(x)], xa_s.at[k - 1], xa_r.at[k - 1], xdev(k))

    def packa_recv(k):
        return remote(packa.at[xrows(xrank(k))], rowsa.at[0, xrows(xrank(NX - k))], xa_s.at[k - 1], xa_r.at[k - 1],
                      xdev(k))

    def pack_b(slot):
        packb[slot, :, 0:DIN] = dot_nn(p_ref[slot], rawb[slot, :, :, 0:DIN].reshape(SPAN, DIN)).astype(BF16)
        packb[slot, :, DIN:WB] = dot_nn(pg_ref[slot], rawb[slot, :, :, DIN:WB].reshape(SPAN, CB)).astype(BF16)

    def send_b(slot):
        for k in (2, 1, 3):
            packb_send(slot, k).start()
        rowsb[slot, xrows(x)] = packb[slot, xrows(x)]

    meta_sib(0, 1 - c).wait_recv()
    build(0)
    cot_sib(1 - c).wait_recv()
    packa[...] = dot_nn(pg_ref[0], rawa[...].reshape(SPAN, WA)).astype(BF16)
    for k in (2, 1, 3):
        packa_send(k).start()
    rowsa[0, xrows(x)] = packa[xrows(x)]

    def raw_pass(step):
        for direction in range(2):
            raw_ring(direction, step - 1).wait_recv()
            if step <= 3:
                raw_ring(direction, step).start()
            if has_meta(direction, step - 1):
                meta_ring(direction, step - 1).wait_recv()
                if step <= 3 and has_meta(direction, step):
                    meta_ring(direction, step).start()
            if step <= 3:
                slot = slots(direction, step - 1)[1]
                raw_sib(slot, c).start()
                meta_sib(slot, c).start()
        if step == 4:
            raw_sib(7, c).start()
            meta_sib(7, c).start()

    def sib_pass(slot):
        raw_sib(slot, 1 - c).wait_recv()
        meta_sib(slot, 1 - c).wait_recv()
        build(slot)
        pack_b(slot)

    def row_start(step, h):
        for direction in range(2):
            if h in row_halves(direction, step):
                row_ring(direction, step, h).start()

    def row_pass(step, h):
        for direction in range(2):
            if h in row_halves(direction, step - 1):
                row_ring(direction, step - 1, h).wait_recv()
                if step <= 3 and h in row_halves(direction, step):
                    row_ring(direction, step, h).start()

    raw_sib(0, 1 - c).wait_recv()
    pack_b(0)
    raw_pass(1)
    loads[4].wait()
    w1b[0] = w1v[...].astype(F32).T.astype(BF16)
    for j in (2, 1, 3):
        w1_send(j).start()
    sib_pass(1)
    sib_pass(2)
    raw_pass(2)
    for k in (1, 3, 2):
        packa_recv(k).wait_recv()
    row_start(0, 0)
    send_b(0)
    send_b(1)
    send_b(2)
    sib_pass(3)
    sib_pass(4)
    raw_pass(3)
    row_start(0, 1)
    send_b(3)
    send_b(4)
    sib_pass(5)
    sib_pass(6)
    send_b(5)
    send_b(6)
    row_pass(1, 0)
    raw_pass(4)
    sib_pass(7)
    send_b(7)
    row_pass(1, 1)

    def forward(s0, n):
        for slot in range(s0, s0 + n):
            for k in (1, 3, 2):
                packb_recv(slot, k).wait_recv()
        rows = slice(s0 * G, (s0 + n) * G)

        @pl.loop(0, 2)
        def _(h):
            w1 = w1b[pl.ds(2 * h, 2)].reshape(HALF, DIN)
            w2 = w2b[pl.ds(2 * h, 2)].reshape(HALF, DOUT)
            pre = dot_nt(rowsb[s0:s0 + n, :, 0:DIN].reshape(n * G, DIN), w1)
            back = dot_nt(rowsb[s0:s0 + n, :, DIN:WB].reshape(n * G, CB), w2[:, 0:CB])
            back += dot_nt(rowsa[s0:s0 + n].reshape(n * G, WA), w2[:, CB:DOUT])
            act, slope = gelu_parts(pre)
            actb[h, rows] = act.astype(BF16)
            bpb[h, rows] = (back * slope).astype(BF16)

        for half in range(2):
            cols = slice(half * 512, (half + 1) * 512)
            part = dot_nn(bpb[0, rows], w1b[0:2, :, cols].reshape(HALF, 512))
            part += dot_nn(bpb[1, rows], w1b[2:4, :, cols].reshape(HALF, 512))
            pown[s0:s0 + n, half] = part.reshape(n, G, 512)

    for j in (1, 3, 2):
        w2_recv(j).wait_recv()
        w1_recv(j).wait_recv()
    forward(0, 1)
    row_pass(2, 0)
    forward(1, 2)
    row_pass(2, 1)
    row_pass(3, 0)
    forward(3, 2)
    row_pass(3, 1)
    forward(5, 2)
    row_pass(4, 0)
    row_pass(4, 1)
    forward(7, 1)

    def rs(direction, step, ch):
        src, dst = sbuf.at[direction, step, ch], rbuf.at[direction, step, ch]
        if step == 0:
            half = pl.ds(direction * (G // 2), G // 2)
            src, dst = src.at[half], dst.at[half]
        return remote(src, dst, rs_s.at[direction, step, ch], rs_r.at[direction, step, ch],
                      right if direction == 0 else left)

    for ch in range(2):
        for direction in range(2):
            half = slice(direction * (G // 2), (direction + 1) * (G // 2))
            sbuf[direction, 0, ch, half] = pown[7, ch, half].astype(BF16)
            rs(direction, 0, ch).start()

    def rs_pass(step):
        for ch in range(2):
            for direction in range(2):
                slot = 7 - 2 * step + direction
                rs(direction, step - 1, ch).wait_recv()
                if step == 1:
                    got = slice(direction * (G // 2), (direction + 1) * (G // 2))
                    rest = slice((1 - direction) * (G // 2), (2 - direction) * (G // 2))
                    sbuf[direction, step, ch, rest] = pown[slot, ch, rest].astype(BF16)
                else:
                    got = slice(0, G)
                sbuf[direction, step, ch, got] = (
                    pown[slot, ch, got] + rbuf[direction, step - 1, ch, got].astype(F32)
                ).astype(BF16)
                rs(direction, step, ch).start()

    def grad_send(j, ch):
        return remote(gsend.at[j - 1, ch], grecv.at[NY - j - 1, ch], gy_s.at[j - 1, ch], gy_r.at[NY - j - 1, ch],
                      (ep, yrank(j)))

    def grad_recv(j, ch):
        return remote(gsend.at[j - 1, ch], grecv.at[j - 1, ch], gy_s.at[j - 1, ch], gy_r.at[j - 1, ch],
                      (ep, yrank(j)))

    def weight_grads(h, ch):
        left_side = bpb[h] if ch == 0 else actb[h]
        for part in range(2):
            col = part * 512
            if ch == 0:
                right_side = rowsb[:, :, col:col + 512]
            elif ch == 1 and part == 0:
                right_side = rowsb[:, :, DIN:WB]
            else:
                at = (ch - 1) * 1024 + col - CB
                right_side = rowsa[:, :, at:at + 512]
            total = dot_tn(left_side, right_side.reshape(ROWS, 512))
            for i in range(2):
                j = 2 * h + i
                block = total[i * SPAN:(i + 1) * SPAN]
                if j == 0:
                    gown[ch, :, col:col + 512] = block
                else:
                    gsend[j - 1, ch, :, col:col + 512] = block.astype(BF16)
        for i in range(2):
            if 2 * h + i:
                grad_send(2 * h + i, ch).start()

    order = (1, 2, 0)
    weight_grads(1, 1)
    weight_grads(1, 2)
    rs_pass(1)
    weight_grads(1, 0)
    weight_grads(0, 1)
    rs_pass(2)
    weight_grads(0, 2)
    weight_grads(0, 0)
    rs_pass(3)

    def ret_send(k):
        return remote(retb.at[xrows(xrank(k))], retr.at[xrows(x)], rt_s.at[k - 1], rt_r.at[k - 1], xdev(k))

    def ret_recv(k):
        return remote(retb.at[xrows(xrank(k))], retr.at[xrows(xrank(NX - k))], rt_s.at[k - 1], rt_r.at[k - 1], xdev(k))

    for ch in range(2):
        for direction in range(2):
            rs(direction, 3, ch).wait_recv()
        retb[:, ch * 512:(ch + 1) * 512] = (
            pown[0, ch] + rbuf[0, 3, ch].astype(F32) + rbuf[1, 3, ch].astype(F32)
        ).astype(BF16)
    for k in (2, 1, 3):
        ret_send(k).start()
    retr[xrows(x)] = retb[xrows(x)]
    for k in (1, 3, 2):
        ret_recv(k).wait_recv()
    sibs[...] = dot_tn(p_ref[0], retr[...]).reshape(NC, QT, DIN)
    other = remote(sibs.at[1 - c], sibr, s2_s.at[0], s2_r.at[0], sibling)
    other.start()
    other.wait_recv()
    total = (sibs[c] + sibr[...]).astype(BF16)
    for q in range(NY):
        giny[q] = total[:, q * QX:(q + 1) * QX]

    def out_send(j):
        return remote(giny.at[yrank(j)], gout.at[quarter], yo_s.at[j - 1], yo_r.at[j - 1], (ep, yrank(j)))

    def out_recv(j):
        return remote(giny.at[yrank(j)], gout.at[pl.ds(pl.multiple_of(yrank(NY - j) * QT, QT), QT)], yo_s.at[j - 1], yo_r.at[j - 1], (ep, yrank(j)))

    for j in (2, 1, 3):
        out_send(j).start()
    gout[quarter] = giny[y]

    stores = [
        pltpu.make_async_copy(gv1, g1_ref.at[0], st.at[0]),
        pltpu.make_async_copy(gv2.at[:, pl.ds(0, 1024)], g2_ref.at[0, :, pl.ds(0, 1024)], st.at[1]),
        pltpu.make_async_copy(gv2.at[:, pl.ds(1024, 1024)], g2_ref.at[0, :, pl.ds(1024, 1024)], st.at[2]),
        pltpu.make_async_copy(gout, gin_ref, st.at[3]),
    ]
    for ch in order:
        for j in (1, 3, 2):
            grad_recv(j, ch).wait_recv()
        total = (
            gown[ch] + grecv[0, ch].astype(F32) + grecv[1, ch].astype(F32) + grecv[2, ch].astype(F32)
        ) * grad_scale
        if ch == 0:
            gv1[...] = total.T.astype(BF16)
            stores[0].start()
        else:
            gv2[:, (ch - 1) * 1024:ch * 1024] = total.astype(BF16)
            stores[ch].start()

    for j in (1, 3, 2):
        out_recv(j).wait_recv()
    stores[3].start()
    for store in stores:
        store.wait()

    for direction in range(2):
        for step in range(4):
            raw_ring(direction, step).wait_send()
            if has_meta(direction, step):
                meta_ring(direction, step).wait_send()
            for h in row_halves(direction, step):
                row_ring(direction, step, h).wait_send()
            for ch in range(2):
                rs(direction, step, ch).wait_send()
    for slot in range(8):
        raw_sib(slot, c).wait_send()
        meta_sib(slot, c).wait_send()
        for k in range(1, NX):
            packb_send(slot, k).wait_send()
    cot_sib(c).wait_send()
    other.wait_send()
    for k in range(1, NX):
        packa_send(k).wait_send()
        ret_send(k).wait_send()
    for j in range(1, NY):
        w1_send(j).wait_send()
        w2_send(j).wait_send()
        out_send(j).wait_send()
        for ch in range(3):
            grad_send(j, ch).wait_send()


def hand_over(a_ref, b_ref, c_ref, a_out, b_out, c_out, a_mid, b_mid, c_mid, sems):
    trios = ((a_ref, a_mid, a_out), (b_ref, b_mid, b_out), (c_ref, c_mid, c_out))
    loads = [pltpu.make_async_copy(src, mid, sems.at[0, i]) for i, (src, mid, _) in enumerate(trios)]
    stores = [pltpu.make_async_copy(mid, dst, sems.at[1, i]) for i, (_, mid, dst) in enumerate(trios)]
    for load in loads:
        load.start()
    for load, store in zip(loads, stores):
        load.wait()
        store.start()
    for store in stores:
        store.wait()


def shards(features, cotangent, expert_ids, gate_levels, w_in, w_out):
    tokens = features.shape[0] * lax.axis_size("ep")
    grad_scale = 1.0 / math.sqrt(2.0 * tokens / E)
    vm = pl.BlockSpec(memory_space=pltpu.VMEM)
    hbm = pl.BlockSpec(memory_space=pl.ANY)
    dma = pltpu.SemaphoreType.DMA

    def pair(*shape):
        return [dma(shape), dma(shape)]

    grads = pl.pallas_call(
        functools.partial(kernel, grad_scale),
        out_shape=(
            jax.ShapeDtypeStruct((TOK, QX), BF16),
            jax.ShapeDtypeStruct((1, DIN, SPAN), BF16),
            jax.ShapeDtypeStruct((1, SPAN, DOUT), BF16),
        ),
        in_specs=[hbm, hbm, vm, vm, hbm, hbm],
        out_specs=(hbm, hbm, hbm),
        scratch_shapes=[
            pltpu.VMEM((NZ, NC, QT, WB), BF16),
            pltpu.VMEM((NC, QT, WA), BF16),
            pltpu.VMEM((NZ, NC, 32, SPAN), BF16),
            pltpu.VMEM((NZ, G, SPAN), BF16),
            pltpu.VMEM((NZ, G, SPAN), BF16),
            pltpu.VMEM((G, WA), BF16),
            pltpu.VMEM((NZ, G, WB), BF16),
            pltpu.VMEM((NZ, G, WA), BF16),
            pltpu.VMEM((NZ, G, WB), BF16),
            pltpu.VMEM((DIN, SPAN), BF16),
            pltpu.VMEM((NY, SPAN, DIN), BF16),
            pltpu.VMEM((NY, SPAN, DOUT), BF16),
            pltpu.VMEM((2, ROWS, HALF), BF16),
            pltpu.VMEM((2, ROWS, HALF), BF16),
            pltpu.VMEM((NZ, 2, G, 512), F32),
            pltpu.VMEM((2, 4, 2, G, 512), BF16),
            pltpu.VMEM((2, 4, 2, G, 512), BF16),
            pltpu.VMEM((3, SPAN, 1024), F32),
            pltpu.VMEM((NY - 1, 3, SPAN, 1024), BF16),
            pltpu.VMEM((NY - 1, 3, SPAN, 1024), BF16),
            pltpu.VMEM((G, DIN), BF16),
            pltpu.VMEM((G, DIN), BF16),
            pltpu.VMEM((NC, QT, DIN), F32),
            pltpu.VMEM((QT, DIN), F32),
            pltpu.VMEM((NY, QT, QX), BF16),
            pltpu.VMEM((TOK, QX), BF16),
            pltpu.VMEM((DIN, SPAN), BF16),
            pltpu.VMEM((SPAN, DOUT), BF16),
            dma((5,)),
            dma((4,)),
            *pair(2, 4), *pair(2, 4), *pair(8), *pair(8), *pair(1),
            *pair(8, 3), *pair(3), *pair(2, 4, 2), *pair(3, 2), *pair(2, 4, 2), *pair(3, 3),
            *pair(3), *pair(1), *pair(3),
        ],
        compiler_params=pltpu.CompilerParams(
            collective_id=0, has_side_effects=True, vmem_limit_bytes=60 * 1024 * 1024
        ),
        cost_estimate=pl.CostEstimate(flops=11_300_000_000, bytes_accessed=5_000_000, transcendentals=0),
        name="moe_backward",
    )(features, cotangent, expert_ids.T, gate_levels.T, w_in, w_out)
    return pl.pallas_call(
        hand_over,
        out_shape=tuple(jax.ShapeDtypeStruct(g.shape, g.dtype) for g in grads),
        in_specs=[hbm] * 3,
        out_specs=(hbm,) * 3,
        scratch_shapes=[*(pltpu.VMEM(g.shape, g.dtype) for g in grads), dma((2, 3))],
        name="hand_over",
    )(*grads)


def solution(mesh):
    return jax.shard_map(
        shards,
        mesh=mesh,
        in_specs=(
            P("ep", None),
            P("ep", None),
            P("ep", None),
            P("ep", None),
            P("ep", None, "tp"),
            P("ep", "tp", None),
        ),
        out_specs=(P("ep", "tp"), P("ep", None, "tp"), P("ep", "tp", None)),
        check_vma=False,
    )
```

time: 610 us -> 123 us (0.20); the launches traced: 600 us -> 123 us
  waiting for transfers between devices: 424 us -> 0 us
  Pallas kernels: 0 us -> 122 us
  local copies, waits for them, and re-layouts: 58.1 us -> 0 us
  starting transfers between devices: 46.3 us -> 0 us
  matrix products: 33.7 us -> 0 us
  other arithmetic: 23 us -> 0 us
  between operations: 15.2 us -> 0.8 us
    ppermute x28 -> x0, waiting for transfers between devices: 372 us -> none  [shifted(): lax.ppermute(value, axis, [(i, (i + by) % peers) for i in range(peers)])]
    pallas_call x0 -> x2, Pallas kernels: none -> 122 us  [the longest x1 120 us: shards(): pl.pallas_call(functools.partial(kernel, grad_scale), out_shape=(jax.Shap...]
    all_to_all x3 -> x0, waiting for transfers between devices: 51.8 us -> none  [the longest x1 32.9 us: shards(): lax.all_to_all(packed_x, 'ep', split_axis=0, concat_axis=0, tiled=True)]
    all_to_all x3 -> x0, starting transfers between devices: 43 us -> none  [the longest x1 22.8 us: shards(): lax.all_to_all(summed.astype(jnp.bfloat16), 'ep', split_axis=1, concat_ax...]
    dot_general x19 -> x0, matrix products: 33.7 us -> none  [the longest x8 10.5 us: span_grads(): lax.dot_general(act_cols, rows_dy, (((0,), (0,)), ((), ())), preferred_el...]
    gather x5 -> x0, local copies, waits for them, and re-layouts: 17.1 us -> none  [the longest x2 5.91 us: shards(): packed_x = features[token_ids] * slot_mask]
    dynamic_update_slice x16 -> x0, local copies, waits for them, and re-layouts: 15.7 us -> none  [the longest x7 7.07 us: shards(): lax.dynamic_update_slice_in_dim(weight_in, moving[0], anchor * span, 1)]
    all_to_all x4 -> x0, local copies, waits for them, and re-layouts: 8.05 us -> none  [the longest x1 4.72 us: shards(): lax.all_to_all(packed_dy, 'ep', split_axis=0, concat_axis=0, tiled=True)]
  transfers between devices with their start and end apart: 32 -> 0, of which waited for: 23 -> 0; matrix products, arithmetic and copies ran while one was open for 12% -> 0% of each run, Pallas kernels for 0% -> 0%
where the time goes in v2:
time: 123 us
  Pallas kernels  122 us (99%)
    pallas_call x1, Pallas kernels, shards(): pl.pallas_call(functools.partial(kernel, grad_scale), out_shape=(jax.Shap...  120 us

profile of v2, /device:TPU:1, one launch (start us, length us, event | category | flops | bytes accessed | tf_op | source)
XLA Modules:
  0.0 122.8 jit_solution(1907467594831958703)
XLA Ops:
  0.6 120.0 %moe_backward.1 = (bf16[256,256]{1,0:T(8,128)(2,1)}, bf16[1,1024,128]{2,1,0:T(8,128)(2,1)}, bf16[1,128,2048]{2,1,0:T(8,128)(2,1)}) custom-call(bf16[256,1024]{1,0:T(8,128)(2,1)} %x_ref.1, bf16[256,2048]{1,0:T(8,128)(2,1)} %dy_ref.1, s32[2,256]{1,0:T(2,128)} %bitcast.2, s32[2,256]{1,0:T(2,128)} %bitcast.3, bf16[1,1024,128]{2,1,0:T(8,128)(2,1)} %w1_ref.1, ...), custom_call_target="tpu_custom_call" | custom-call | flops 11299999744 | bytes 5000000 | tf_op jit(solution)/shard_map/moe_backward/pallas_call | solution.py:528
  120.6 2.0 %hand_over.1 = (bf16[256,256]{1,0:T(8,128)(2,1)}, bf16[1,1024,128]{2,1,0:T(8,128)(2,1)}, bf16[1,128,2048]{2,1,0:T(8,128)(2,1)}) custom-call(bf16[256,256]{1,0:T(8,128)(2,1)} %get-tuple-element.6.a_ref, bf16[1,1024,128]{2,1,0:T(8,128)(2,1)} %get-tuple-element.7.b_ref, bf16[1,128,2048]{2,1,0:T(8,128)(2,1)} %get-tuple-element.8.c_ref), custom_call_target="tpu_custom_call" | custom-call | tf_op jit(solution)/shard_map/hand_over/pallas_call | solution.py:578

commit v3 on v2

--- a/solution.py
+++ b/solution.py
@@ -52,14 +52,14 @@
 
 def kernel(
     grad_scale,
-    x_ref, dy_ref, ids_ref, gate_ref, w1_ref, w2_ref,
+    x_ref, dy_ref, ids_hbm, gate_hbm, w1_ref, w2_ref,
     gin_ref, g1_ref, g2_ref,
-    rawb, rawa, meta, p_ref, pg_ref, packa, packb, rowsa, rowsb,
-    w1v, w1b, w2b, actb, bpb, pown, sbuf, rbuf, gown, gsend, grecv,
-    retb, retr, sibs, sibr, giny, gout, gv1, gv2,
+    rawb, rawa, meta, p_ref, pg_ref, p_all, packa, packb, rowsa, rowsb,
+    ids_ref, gate_ref, w1v, w1b, w2b, actb, bpb, pown, sbuf, rbuf, gown, gfar, gnear, ghalf, gsend, grecv,
+    retb, retr, tokens, giny, gout, gv1, gv2,
     ld, st, zb_s, zb_r, zm_s, zm_r, sb_s, sb_r, sm_s, sm_r, sa_s, sa_r,
-    xb_s, xb_r, xa_s, xa_r, za_s, za_r, wy_s, wy_r, rs_s, rs_r, gy_s, gy_r,
-    rt_s, rt_r, s2_s, s2_r, yo_s, yo_r,
+    xb_s, xb_r, xa_s, xa_r, za_s, za_r, wy_s, wy_r, rs_s, rs_r, gh_s, gh_r, gy_s, gy_r,
+    rt_s, rt_r, yo_s, yo_r,
 ):
     ep = lax.axis_index("ep")
     y = lax.axis_index("tp")
@@ -80,6 +80,9 @@
     def yrank(k):
         return lax.rem(y + k, NY)
 
+    def plane(m):
+        return (z * E + lax.rem(me + m, E), y)
+
     def remote(src, dst, ss, rs, dev):
         return pltpu.make_async_remote_copy(
             src_ref=src, dst_ref=dst, send_sem=ss, recv_sem=rs, device_id=dev, device_id_type=MESH
@@ -92,13 +95,15 @@
         pltpu.make_async_copy(dy_ref.at[quarter, pl.ds(CB, WA)], rawa.at[c], ld.at[2]),
         pltpu.make_async_copy(w2_ref.at[0], w2b.at[0], ld.at[3]),
         pltpu.make_async_copy(w1_ref.at[0], w1v, ld.at[4]),
+        pltpu.make_async_copy(ids_hbm, ids_ref, ld.at[5]),
+        pltpu.make_async_copy(gate_hbm, gate_ref, ld.at[6]),
     ]
     for load in loads:
         load.start()
 
     bar = pltpu.get_barrier_semaphore()
-    partners = [left, right, sibling]
-    partners += [xdev(k) for k in range(1, NX)] + [(ep, yrank(k)) for k in range(1, NY)]
+    partners = [left, right]
+    partners += [plane(m) for m in range(1, E)] + [(ep, yrank(k)) for k in range(1, NY)]
     for dev in partners:
         pl.semaphore_signal(bar, inc=1, device_id=dev, device_id_type=MESH)
     pl.semaphore_wait(bar, len(partners))
@@ -126,14 +131,16 @@
     def has_meta(direction, step):
         return step < 3 or direction == 0
 
-    def row_ring(direction, step, h):
+    def row_ring(direction, step, k):
         s, d = slots(direction, step)
-        half = pl.ds(h * (G // 2), G // 2)
-        return remote(rowsa.at[s, half], rowsa.at[d, half], za_s.at[direction, step, h], za_r.at[direction, step, h],
+        piece = pl.ds(pl.multiple_of(xrank(k) * SL, 16), SL)
+        return remote(rowsa.at[s, piece], rowsa.at[d, piece], za_s.at[direction, step, k], za_r.at[direction, step, k],
                       toward(direction))
 
-    def row_halves(direction, step):
-        return (direction,) if step == 3 else (0, 1)
+    def row_pieces(direction, step):
+        if step == 3:
+            return (0, 2) if direction == 0 else (1, 3)
+        return (0, 1, 3, 2)
 
     def raw_sib(slot, core):
         return remote(rawb.at[slot, core], rawb.at[slot, core], sb_s.at[slot], sb_r.at[slot], sibling)
@@ -152,6 +159,8 @@
     for direction in range(2):
         raw_ring(direction, 0).start()
 
+    loads[5].wait()
+    loads[6].wait()
     expert = lax.broadcasted_iota(jnp.int32, (16, TOK), 0)
     first = jnp.broadcast_to(ids_ref[0:1], (16, TOK)) == expert
     second = jnp.broadcast_to(ids_ref[1:2], (16, TOK)) == expert
@@ -199,7 +208,13 @@
             row = jnp.where(c == 0, both[2 * k:2 * k + 1], both[2 * k + 1:2 * k + 2])
             gate = jnp.where(c == 0, both[16 + 2 * k:17 + 2 * k], both[17 + 2 * k:18 + 2 * k])
             hit = jnp.broadcast_to(row, (SL, SPAN)) == want
-            p_ref[slot, k * SL:(k + 1) * SL] = jnp.where(hit, 1.0, 0.0).astype(BF16)
+            chosen = jnp.where(hit, 1.0, 0.0).astype(BF16)
+            p_ref[slot, k * SL:(k + 1) * SL] = chosen
+            if slot == 0:
+                p_all[0, k * SL:(k + 1) * SL] = chosen
+                row = jnp.where(c == 0, both[2 * k + 1:2 * k + 2], both[2 * k:2 * k + 1])
+                chosen = jnp.where(jnp.broadcast_to(row, (SL, SPAN)) == want, 1.0, 0.0).astype(BF16)
+                p_all[1, k * SL:(k + 1) * SL] = chosen
             pg_ref[slot, k * SL:(k + 1) * SL] = jnp.where(
                 hit, jnp.broadcast_to(gate, (SL, SPAN)), 0.0).astype(BF16)
 
@@ -234,7 +249,7 @@
     build(0)
     cot_sib(1 - c).wait_recv()
     packa[...] = dot_nn(pg_ref[0], rawa[...].reshape(SPAN, WA)).astype(BF16)
-    for k in (2, 1, 3):
+    for k in (1, 3, 2):
         packa_send(k).start()
     rowsa[0, xrows(x)] = packa[xrows(x)]
 
@@ -261,49 +276,55 @@
         build(slot)
         pack_b(slot)
 
-    def row_start(step, h):
+    def row_start(k):
         for direction in range(2):
-            if h in row_halves(direction, step):
-                row_ring(direction, step, h).start()
-
-    def row_pass(step, h):
+            row_ring(direction, 0, k).start()
+
+    def row_pass(step, k):
         for direction in range(2):
-            if h in row_halves(direction, step - 1):
-                row_ring(direction, step - 1, h).wait_recv()
-                if step <= 3 and h in row_halves(direction, step):
-                    row_ring(direction, step, h).start()
-
+            if k in row_pieces(direction, step - 1):
+                row_ring(direction, step - 1, k).wait_recv()
+                if step <= 3 and k in row_pieces(direction, step):
+                    row_ring(direction, step, k).start()
+
+    row_start(0)
+    raw_pass(1)
     raw_sib(0, 1 - c).wait_recv()
     pack_b(0)
-    raw_pass(1)
+    packa_recv(3).wait_recv()
+    row_start(1)
+    packa_recv(1).wait_recv()
+    row_start(3)
+    send_b(0)
+    sib_pass(1)
+    sib_pass(2)
+    send_b(1)
+    send_b(2)
+    packa_recv(2).wait_recv()
+    row_start(2)
+    raw_pass(2)
     loads[4].wait()
     w1b[0] = w1v[...].astype(F32).T.astype(BF16)
     for j in (2, 1, 3):
         w1_send(j).start()
-    sib_pass(1)
-    sib_pass(2)
-    raw_pass(2)
-    for k in (1, 3, 2):
-        packa_recv(k).wait_recv()
-    row_start(0, 0)
-    send_b(0)
-    send_b(1)
-    send_b(2)
     sib_pass(3)
     sib_pass(4)
-    raw_pass(3)
-    row_start(0, 1)
     send_b(3)
     send_b(4)
+    row_pass(1, 0)
+    raw_pass(3)
+    row_pass(1, 1)
     sib_pass(5)
     sib_pass(6)
     send_b(5)
     send_b(6)
-    row_pass(1, 0)
+    row_pass(1, 3)
     raw_pass(4)
+    row_pass(1, 2)
     sib_pass(7)
     send_b(7)
-    row_pass(1, 1)
+    row_pass(2, 0)
+    row_pass(2, 1)
 
     def forward(s0, n):
         for slot in range(s0, s0 + n):
@@ -322,25 +343,27 @@
             actb[h, rows] = act.astype(BF16)
             bpb[h, rows] = (back * slope).astype(BF16)
 
-        for half in range(2):
-            cols = slice(half * 512, (half + 1) * 512)
-            part = dot_nn(bpb[0, rows], w1b[0:2, :, cols].reshape(HALF, 512))
-            part += dot_nn(bpb[1, rows], w1b[2:4, :, cols].reshape(HALF, 512))
-            pown[s0:s0 + n, half] = part.reshape(n, G, 512)
+        for q in range(NY):
+            cols = slice(q * QX, (q + 1) * QX)
+            part = dot_nn(bpb[0, rows], w1b[0:2, :, cols].reshape(HALF, QX))
+            part += dot_nn(bpb[1, rows], w1b[2:4, :, cols].reshape(HALF, QX))
+            pown[s0:s0 + n, q] = part.reshape(n, G, QX)
 
     for j in (1, 3, 2):
         w2_recv(j).wait_recv()
         w1_recv(j).wait_recv()
     forward(0, 1)
-    row_pass(2, 0)
+    row_pass(2, 3)
+    row_pass(2, 2)
+    row_pass(3, 0)
     forward(1, 2)
-    row_pass(2, 1)
-    row_pass(3, 0)
+    row_pass(3, 1)
+    row_pass(3, 3)
+    row_pass(3, 2)
     forward(3, 2)
-    row_pass(3, 1)
     forward(5, 2)
-    row_pass(4, 0)
-    row_pass(4, 1)
+    for k in range(NX):
+        row_pass(4, k)
     forward(7, 1)
 
     def rs(direction, step, ch):
@@ -351,35 +374,47 @@
         return remote(src, dst, rs_s.at[direction, step, ch], rs_r.at[direction, step, ch],
                       right if direction == 0 else left)
 
-    for ch in range(2):
+    turns = [yrank(j) for j in (2, 1, 3, 0)]
+    for ch in turns:
         for direction in range(2):
             half = slice(direction * (G // 2), (direction + 1) * (G // 2))
             sbuf[direction, 0, ch, half] = pown[7, ch, half].astype(BF16)
             rs(direction, 0, ch).start()
 
-    def rs_pass(step):
-        for ch in range(2):
-            for direction in range(2):
-                slot = 7 - 2 * step + direction
-                rs(direction, step - 1, ch).wait_recv()
-                if step == 1:
-                    got = slice(direction * (G // 2), (direction + 1) * (G // 2))
-                    rest = slice((1 - direction) * (G // 2), (2 - direction) * (G // 2))
-                    sbuf[direction, step, ch, rest] = pown[slot, ch, rest].astype(BF16)
-                else:
-                    got = slice(0, G)
-                sbuf[direction, step, ch, got] = (
-                    pown[slot, ch, got] + rbuf[direction, step - 1, ch, got].astype(F32)
-                ).astype(BF16)
-                rs(direction, step, ch).start()
-
-    def grad_send(j, ch):
-        return remote(gsend.at[j - 1, ch], grecv.at[NY - j - 1, ch], gy_s.at[j - 1, ch], gy_r.at[NY - j - 1, ch],
-                      (ep, yrank(j)))
-
-    def grad_recv(j, ch):
-        return remote(gsend.at[j - 1, ch], grecv.at[j - 1, ch], gy_s.at[j - 1, ch], gy_r.at[j - 1, ch],
-                      (ep, yrank(j)))
+    def rs_pass(step, ch):
+        for direction in range(2):
+            slot = 7 - 2 * step + direction
+            rs(direction, step - 1, ch).wait_recv()
+            if step == 1:
+                got = slice(direction * (G // 2), (direction + 1) * (G // 2))
+                rest = slice((1 - direction) * (G // 2), (2 - direction) * (G // 2))
+                sbuf[direction, step, ch, rest] = pown[slot, ch, rest].astype(BF16)
+            else:
+                got = slice(0, G)
+            sbuf[direction, step, ch, got] = (
+                pown[slot, ch, got] + rbuf[direction, step - 1, ch, got].astype(F32)
+            ).astype(BF16)
+            rs(direction, step, ch).start()
+
+    ways = (1, NY - 1)
+
+    def half_rows(way):
+        return pl.ds(way * (SPAN // 2), SPAN // 2)
+
+    def grad_half(way, ch):
+        return remote(gfar.at[ch, half_rows(way)], ghalf.at[ch, half_rows(way)], gh_s.at[way, ch], gh_r.at[way, ch],
+                      (ep, yrank(ways[way])))
+
+    def grad_send(way, ch):
+        return remote(gsend.at[way, ch], grecv.at[way, ch], gy_s.at[way, ch], gy_r.at[way, ch], (ep, yrank(ways[way])))
+
+    def grad_near(way, ch):
+        grad_half(way, ch).wait_recv()
+        got = half_rows(way)
+        rest = half_rows(1 - way)
+        gsend[way, ch, rest] = gnear[way, ch, rest].astype(BF16)
+        gsend[way, ch, got] = (gnear[way, ch, got] + ghalf[ch, got].astype(F32)).astype(BF16)
+        grad_send(way, ch).start()
 
     def weight_grads(h, ch):
         left_side = bpb[h] if ch == 0 else actb[h]
@@ -398,57 +433,71 @@
                 block = total[i * SPAN:(i + 1) * SPAN]
                 if j == 0:
                     gown[ch, :, col:col + 512] = block
+                elif j == 2:
+                    gfar[ch, :, col:col + 512] = block.astype(BF16)
                 else:
-                    gsend[j - 1, ch, :, col:col + 512] = block.astype(BF16)
-        for i in range(2):
-            if 2 * h + i:
-                grad_send(2 * h + i, ch).start()
-
-    order = (1, 2, 0)
+                    gnear[j // 2, ch, :, col:col + 512] = block
+        for way in range(2):
+            if h == 1:
+                grad_half(way, ch).start()
+            else:
+                grad_near(way, ch)
+
     weight_grads(1, 1)
+    rs_pass(1, turns[0])
     weight_grads(1, 2)
-    rs_pass(1)
+    rs_pass(1, turns[1])
+    rs_pass(1, turns[2])
     weight_grads(1, 0)
+    rs_pass(1, turns[3])
     weight_grads(0, 1)
-    rs_pass(2)
+    rs_pass(2, turns[0])
     weight_grads(0, 2)
+    rs_pass(2, turns[1])
     weight_grads(0, 0)
-    rs_pass(3)
-
-    def ret_send(k):
-        return remote(retb.at[xrows(xrank(k))], retr.at[xrows(x)], rt_s.at[k - 1], rt_r.at[k - 1], xdev(k))
-
-    def ret_recv(k):
-        return remote(retb.at[xrows(xrank(k))], retr.at[xrows(xrank(NX - k))], rt_s.at[k - 1], rt_r.at[k - 1], xdev(k))
-
-    for ch in range(2):
+    rs_pass(2, turns[2])
+    rs_pass(2, turns[3])
+    for ch in turns:
+        rs_pass(3, ch)
+
+    def ret_send(m, ch):
+        to = lax.rem(me + m, E) // NC
+        return remote(retb.at[ch, xrows(to)], retr.at[ch, m % 2, xrows(x)], rt_s.at[m - 1, ch], rt_r.at[m - 1, ch],
+                      plane(m))
+
+    def ret_recv(m, ch):
+        source = lax.rem(me + E - m, E) // NC
+        return remote(retb.at[ch, xrows(x)], retr.at[ch, m % 2, xrows(source)], rt_s.at[m - 1, ch], rt_r.at[m - 1, ch],
+                      plane(m))
+
+    def out_send(j):
+        return remote(giny.at[yrank(j)], gout.at[quarter], yo_s.at[j - 1], yo_r.at[j - 1], (ep, yrank(j)))
+
+    def out_recv(j):
+        return remote(giny.at[yrank(j)], gout.at[pl.ds(pl.multiple_of(yrank(NY - j) * QT, QT), QT)], yo_s.at[j - 1],
+                      yo_r.at[j - 1], (ep, yrank(j)))
+
+    far_first = (4, 3, 5, 2, 6, 1, 7)
+
+    def tail_rows(j):
+        ch = yrank(j)
         for direction in range(2):
             rs(direction, 3, ch).wait_recv()
-        retb[:, ch * 512:(ch + 1) * 512] = (
-            pown[0, ch] + rbuf[0, 3, ch].astype(F32) + rbuf[1, 3, ch].astype(F32)
-        ).astype(BF16)
-    for k in (2, 1, 3):
-        ret_send(k).start()
-    retr[xrows(x)] = retb[xrows(x)]
-    for k in (1, 3, 2):
-        ret_recv(k).wait_recv()
-    sibs[...] = dot_tn(p_ref[0], retr[...]).reshape(NC, QT, DIN)
-    other = remote(sibs.at[1 - c], sibr, s2_s.at[0], s2_r.at[0], sibling)
-    other.start()
-    other.wait_recv()
-    total = (sibs[c] + sibr[...]).astype(BF16)
-    for q in range(NY):
-        giny[q] = total[:, q * QX:(q + 1) * QX]
-
-    def out_send(j):
-        return remote(giny.at[yrank(j)], gout.at[quarter], yo_s.at[j - 1], yo_r.at[j - 1], (ep, yrank(j)))
-
-    def out_recv(j):
-        return remote(giny.at[yrank(j)], gout.at[pl.ds(pl.multiple_of(yrank(NY - j) * QT, QT), QT)], yo_s.at[j - 1], yo_r.at[j - 1], (ep, yrank(j)))
-
-    for j in (2, 1, 3):
-        out_send(j).start()
-    gout[quarter] = giny[y]
+        retb[ch] = (pown[0, ch] + rbuf[0, 3, ch].astype(F32) + rbuf[1, 3, ch].astype(F32)).astype(BF16)
+        for m in far_first:
+            ret_send(m, ch).start()
+        retr[ch, 0, xrows(x)] = retb[ch, xrows(x)]
+
+    def tail_tokens(j):
+        ch = yrank(j)
+        for m in far_first:
+            ret_recv(m, ch).wait_recv()
+        tokens[...] = dot_tn(p_all[...].reshape(2 * G, SPAN), retr[ch].reshape(2 * G, QX)).reshape(NC, QT, QX)
+        if j:
+            giny[ch] = tokens[c].astype(BF16)
+            out_send(j).start()
+        else:
+            gout[quarter] = tokens[c].astype(BF16)
 
     stores = [
         pltpu.make_async_copy(gv1, g1_ref.at[0], st.at[0]),
@@ -456,19 +505,28 @@
         pltpu.make_async_copy(gv2.at[:, pl.ds(1024, 1024)], g2_ref.at[0, :, pl.ds(1024, 1024)], st.at[2]),
         pltpu.make_async_copy(gout, gin_ref, st.at[3]),
     ]
-    for ch in order:
-        for j in (1, 3, 2):
-            grad_recv(j, ch).wait_recv()
-        total = (
-            gown[ch] + grecv[0, ch].astype(F32) + grecv[1, ch].astype(F32) + grecv[2, ch].astype(F32)
-        ) * grad_scale
+
+    def finish(ch):
+        for way in range(2):
+            grad_send(way, ch).wait_recv()
+        total = (gown[ch] + grecv[0, ch].astype(F32) + grecv[1, ch].astype(F32)) * grad_scale
         if ch == 0:
             gv1[...] = total.T.astype(BF16)
-            stores[0].start()
         else:
             gv2[:, (ch - 1) * 1024:ch * 1024] = total.astype(BF16)
-            stores[ch].start()
-
+        stores[ch].start()
+
+    finish(1)
+    tail_rows(2)
+    finish(2)
+    tail_rows(1)
+    tail_tokens(2)
+    finish(0)
+    tail_rows(3)
+    tail_tokens(1)
+    tail_rows(0)
+    tail_tokens(3)
+    tail_tokens(0)
     for j in (1, 3, 2):
         out_recv(j).wait_recv()
     stores[3].start()
@@ -480,9 +538,9 @@
             raw_ring(direction, step).wait_send()
             if has_meta(direction, step):
                 meta_ring(direction, step).wait_send()
-            for h in row_halves(direction, step):
-                row_ring(direction, step, h).wait_send()
-            for ch in range(2):
+            for k in row_pieces(direction, step):
+                row_ring(direction, step, k).wait_send()
+            for ch in range(NY):
                 rs(direction, step, ch).wait_send()
     for slot in range(8):
         raw_sib(slot, c).wait_send()
@@ -490,16 +548,19 @@
         for k in range(1, NX):
             packb_send(slot, k).wait_send()
     cot_sib(c).wait_send()
-    other.wait_send()
     for k in range(1, NX):
         packa_send(k).wait_send()
-        ret_send(k).wait_send()
+    for m in range(1, E):
+        for ch in range(NY):
+            ret_send(m, ch).wait_send()
     for j in range(1, NY):
         w1_send(j).wait_send()
         w2_send(j).wait_send()
         out_send(j).wait_send()
+    for way in range(2):
         for ch in range(3):
-            grad_send(j, ch).wait_send()
+            grad_half(way, ch).wait_send()
+            grad_send(way, ch).wait_send()
 
 
 def hand_over(a_ref, b_ref, c_ref, a_out, b_out, c_out, a_mid, b_mid, c_mid, sems):
@@ -518,7 +579,6 @@
 def shards(features, cotangent, expert_ids, gate_levels, w_in, w_out):
     tokens = features.shape[0] * lax.axis_size("ep")
     grad_scale = 1.0 / math.sqrt(2.0 * tokens / E)
-    vm = pl.BlockSpec(memory_space=pltpu.VMEM)
     hbm = pl.BlockSpec(memory_space=pl.ANY)
     dma = pltpu.SemaphoreType.DMA
 
@@ -532,7 +592,7 @@
             jax.ShapeDtypeStruct((1, DIN, SPAN), BF16),
             jax.ShapeDtypeStruct((1, SPAN, DOUT), BF16),
         ),
-        in_specs=[hbm, hbm, vm, vm, hbm, hbm],
+        in_specs=[hbm] * 6,
         out_specs=(hbm, hbm, hbm),
         scratch_shapes=[
             pltpu.VMEM((NZ, NC, QT, WB), BF16),
@@ -540,34 +600,39 @@
             pltpu.VMEM((NZ, NC, 32, SPAN), BF16),
             pltpu.VMEM((NZ, G, SPAN), BF16),
             pltpu.VMEM((NZ, G, SPAN), BF16),
+            pltpu.VMEM((2, G, SPAN), BF16),
             pltpu.VMEM((G, WA), BF16),
             pltpu.VMEM((NZ, G, WB), BF16),
             pltpu.VMEM((NZ, G, WA), BF16),
             pltpu.VMEM((NZ, G, WB), BF16),
+            pltpu.VMEM((2, TOK), jnp.int32),
+            pltpu.VMEM((2, TOK), jnp.int32),
             pltpu.VMEM((DIN, SPAN), BF16),
             pltpu.VMEM((NY, SPAN, DIN), BF16),
             pltpu.VMEM((NY, SPAN, DOUT), BF16),
             pltpu.VMEM((2, ROWS, HALF), BF16),
             pltpu.VMEM((2, ROWS, HALF), BF16),
-            pltpu.VMEM((NZ, 2, G, 512), F32),
-            pltpu.VMEM((2, 4, 2, G, 512), BF16),
-            pltpu.VMEM((2, 4, 2, G, 512), BF16),
+            pltpu.VMEM((NZ, NY, G, QX), F32),
+            pltpu.VMEM((2, 4, NY, G, QX), BF16),
+            pltpu.VMEM((2, 4, NY, G, QX), BF16),
             pltpu.VMEM((3, SPAN, 1024), F32),
-            pltpu.VMEM((NY - 1, 3, SPAN, 1024), BF16),
-            pltpu.VMEM((NY - 1, 3, SPAN, 1024), BF16),
-            pltpu.VMEM((G, DIN), BF16),
-            pltpu.VMEM((G, DIN), BF16),
-            pltpu.VMEM((NC, QT, DIN), F32),
-            pltpu.VMEM((QT, DIN), F32),
+            pltpu.VMEM((3, SPAN, 1024), BF16),
+            pltpu.VMEM((2, 3, SPAN, 1024), F32),
+            pltpu.VMEM((3, SPAN, 1024), BF16),
+            pltpu.VMEM((2, 3, SPAN, 1024), BF16),
+            pltpu.VMEM((2, 3, SPAN, 1024), BF16),
+            pltpu.VMEM((NY, G, QX), BF16),
+            pltpu.VMEM((NY, 2, G, QX), BF16),
+            pltpu.VMEM((NC, QT, QX), F32),
             pltpu.VMEM((NY, QT, QX), BF16),
             pltpu.VMEM((TOK, QX), BF16),
             pltpu.VMEM((DIN, SPAN), BF16),
             pltpu.VMEM((SPAN, DOUT), BF16),
-            dma((5,)),
+            dma((7,)),
             dma((4,)),
             *pair(2, 4), *pair(2, 4), *pair(8), *pair(8), *pair(1),
-            *pair(8, 3), *pair(3), *pair(2, 4, 2), *pair(3, 2), *pair(2, 4, 2), *pair(3, 3),
-            *pair(3), *pair(1), *pair(3),
+            *pair(8, 3), *pair(3), *pair(2, 4, NX), *pair(3, 2), *pair(2, 4, NY), *pair(2, 3), *pair(2, 3),
+            *pair(E - 1, NY), *pair(3),
         ],
         compiler_params=pltpu.CompilerParams(
             collective_id=0, has_side_effects=True, vmem_limit_bytes=60 * 1024 * 1024

time: 123 us -> 119 us (0.967)
  Pallas kernels: 122 us -> 117 us
    pallas_call x1, Pallas kernels: 120 us -> 115 us  [shards(): pl.pallas_call(functools.partial(kernel, grad_scale), out_shape=(jax.Shap...]
where the time goes in v3:
time: 119 us; the launch traced here: 118 us
  Pallas kernels  117 us (98%)
    pallas_call x1, Pallas kernels, shards(): pl.pallas_call(functools.partial(kernel, grad_scale), out_shape=(jax.Shap...  115 us

profile of v3, /device:TPU:1, one launch (start us, length us, event | category | flops | bytes accessed | tf_op | source)
XLA Modules:
  0.0 118.1 jit_solution(14379085543080139301)
XLA Ops:
  0.6 115.3 %moe_backward.1 = (bf16[256,256]{1,0:T(8,128)(2,1)}, bf16[1,1024,128]{2,1,0:T(8,128)(2,1)}, bf16[1,128,2048]{2,1,0:T(8,128)(2,1)}) custom-call(bf16[256,1024]{1,0:T(8,128)(2,1)} %x_ref.1, bf16[256,2048]{1,0:T(8,128)(2,1)} %dy_ref.1, s32[2,256]{1,0:T(2,128)} %bitcast.2, s32[2,256]{1,0:T(2,128)} %bitcast.3, bf16[1,1024,128]{2,1,0:T(8,128)(2,1)} %w1_ref.1, ...), custom_call_target="tpu_custom_call" | custom-call | flops 11299999744 | bytes 5000000 | tf_op jit(solution)/shard_map/moe_backward/pallas_call | solution.py:588
  115.9 2.0 %hand_over.1 = (bf16[256,256]{1,0:T(8,128)(2,1)}, bf16[1,1024,128]{2,1,0:T(8,128)(2,1)}, bf16[1,128,2048]{2,1,0:T(8,128)(2,1)}) custom-call(bf16[256,256]{1,0:T(8,128)(2,1)} %get-tuple-element.6.a_ref, bf16[1,1024,128]{2,1,0:T(8,128)(2,1)} %get-tuple-element.7.b_ref, bf16[1,128,2048]{2,1,0:T(8,128)(2,1)} %get-tuple-element.8.c_ref), custom_call_target="tpu_custom_call" | custom-call | tf_op jit(solution)/shard_map/hand_over/pallas_call | solution.py:643

commit v4 on v3

--- a/solution.py
+++ b/solution.py
@@ -18,6 +18,7 @@
 SPAN = 128
 QX = DIN // NY
 SL = 48
+RB = 32
 G = NX * SL
 CB = 512
 WB = DIN + CB
@@ -56,8 +57,8 @@
     gin_ref, g1_ref, g2_ref,
     rawb, rawa, meta, p_ref, pg_ref, p_all, packa, packb, rowsa, rowsb,
     ids_ref, gate_ref, w1v, w1b, w2b, actb, bpb, pown, sbuf, rbuf, gown, gfar, gnear, ghalf, gsend, grecv,
-    retb, retr, tokens, giny, gout, gv1, gv2,
-    ld, st, zb_s, zb_r, zm_s, zm_r, sb_s, sb_r, sm_s, sm_r, sa_s, sa_r,
+    retb, retr, tokens, giny, gout,
+    ld, zb_s, zb_r, zm_s, zm_r, sb_s, sb_r, sm_s, sm_r, sa_s, sa_r,
     xb_s, xb_r, xa_s, xa_r, za_s, za_r, wy_s, wy_r, rs_s, rs_r, gh_s, gh_r, gy_s, gy_r,
     rt_s, rt_r, yo_s, yo_r,
 ):
@@ -211,10 +212,11 @@
             chosen = jnp.where(hit, 1.0, 0.0).astype(BF16)
             p_ref[slot, k * SL:(k + 1) * SL] = chosen
             if slot == 0:
-                p_all[0, k * SL:(k + 1) * SL] = chosen
-                row = jnp.where(c == 0, both[2 * k + 1:2 * k + 2], both[2 * k:2 * k + 1])
-                chosen = jnp.where(jnp.broadcast_to(row, (SL, SPAN)) == want, 1.0, 0.0).astype(BF16)
-                p_all[1, k * SL:(k + 1) * SL] = chosen
+                back = lax.broadcasted_iota(jnp.int32, (RB, SPAN), 0).astype(F32) + jnp.where(c == 0, 1.0, 17.0)
+                swap = jnp.where(c == 0, both[2 * k + 1:2 * k + 2], both[2 * k:2 * k + 1])
+                for i, line in enumerate((row, swap)):
+                    p_all[i, k * RB:(k + 1) * RB] = jnp.where(
+                        jnp.broadcast_to(line, (RB, SPAN)) == back, 1.0, 0.0).astype(BF16)
             pg_ref[slot, k * SL:(k + 1) * SL] = jnp.where(
                 hit, jnp.broadcast_to(gate, (SL, SPAN)), 0.0).astype(BF16)
 
@@ -460,15 +462,21 @@
     for ch in turns:
         rs_pass(3, ch)
 
+    def rows_for(chip, core):
+        return pl.ds(pl.multiple_of(chip * SL + core * (SL - RB), 16), RB)
+
+    def rows_from(chip):
+        return pl.ds(pl.multiple_of(chip * RB, RB), RB)
+
     def ret_send(m, ch):
-        to = lax.rem(me + m, E) // NC
-        return remote(retb.at[ch, xrows(to)], retr.at[ch, m % 2, xrows(x)], rt_s.at[m - 1, ch], rt_r.at[m - 1, ch],
-                      plane(m))
+        to = lax.rem(me + m, E)
+        return remote(retb.at[ch, rows_for(to // NC, lax.rem(to, NC))], retr.at[ch, m % 2, rows_from(x)],
+                      rt_s.at[m - 1, ch], rt_r.at[m - 1, ch], plane(m))
 
     def ret_recv(m, ch):
-        source = lax.rem(me + E - m, E) // NC
-        return remote(retb.at[ch, xrows(x)], retr.at[ch, m % 2, xrows(source)], rt_s.at[m - 1, ch], rt_r.at[m - 1, ch],
-                      plane(m))
+        source = lax.rem(me + E - m, E)
+        return remote(retb.at[ch, rows_for(x, c)], retr.at[ch, m % 2, rows_from(source // NC)],
+                      rt_s.at[m - 1, ch], rt_r.at[m - 1, ch], plane(m))
 
     def out_send(j):
         return remote(giny.at[yrank(j)], gout.at[quarter], yo_s.at[j - 1], yo_r.at[j - 1], (ep, yrank(j)))
@@ -486,35 +494,27 @@
         retb[ch] = (pown[0, ch] + rbuf[0, 3, ch].astype(F32) + rbuf[1, 3, ch].astype(F32)).astype(BF16)
         for m in far_first:
             ret_send(m, ch).start()
-        retr[ch, 0, xrows(x)] = retb[ch, xrows(x)]
+        retr[ch, 0, rows_from(x)] = retb[ch, rows_for(x, c)]
 
     def tail_tokens(j):
         ch = yrank(j)
         for m in far_first:
             ret_recv(m, ch).wait_recv()
-        tokens[...] = dot_tn(p_all[...].reshape(2 * G, SPAN), retr[ch].reshape(2 * G, QX)).reshape(NC, QT, QX)
+        tokens[...] = dot_tn(p_all[...].reshape(2 * NX * RB, SPAN), retr[ch].reshape(2 * NX * RB, QX)).reshape(NC, QT, QX)
         if j:
             giny[ch] = tokens[c].astype(BF16)
             out_send(j).start()
         else:
             gout[quarter] = tokens[c].astype(BF16)
 
-    stores = [
-        pltpu.make_async_copy(gv1, g1_ref.at[0], st.at[0]),
-        pltpu.make_async_copy(gv2.at[:, pl.ds(0, 1024)], g2_ref.at[0, :, pl.ds(0, 1024)], st.at[1]),
-        pltpu.make_async_copy(gv2.at[:, pl.ds(1024, 1024)], g2_ref.at[0, :, pl.ds(1024, 1024)], st.at[2]),
-        pltpu.make_async_copy(gout, gin_ref, st.at[3]),
-    ]
-
     def finish(ch):
         for way in range(2):
             grad_send(way, ch).wait_recv()
         total = (gown[ch] + grecv[0, ch].astype(F32) + grecv[1, ch].astype(F32)) * grad_scale
         if ch == 0:
-            gv1[...] = total.T.astype(BF16)
+            g1_ref[0] = total.T.astype(BF16)
         else:
-            gv2[:, (ch - 1) * 1024:ch * 1024] = total.astype(BF16)
-        stores[ch].start()
+            g2_ref[0, :, (ch - 1) * 1024:ch * 1024] = total.astype(BF16)
 
     finish(1)
     tail_rows(2)
@@ -529,9 +529,7 @@
     tail_tokens(0)
     for j in (1, 3, 2):
         out_recv(j).wait_recv()
-    stores[3].start()
-    for store in stores:
-        store.wait()
+    gin_ref[...] = gout[...]
 
     for direction in range(2):
         for step in range(4):
@@ -563,23 +561,22 @@
             grad_send(way, ch).wait_send()
 
 
-def hand_over(a_ref, b_ref, c_ref, a_out, b_out, c_out, a_mid, b_mid, c_mid, sems):
-    trios = ((a_ref, a_mid, a_out), (b_ref, b_mid, b_out), (c_ref, c_mid, c_out))
-    loads = [pltpu.make_async_copy(src, mid, sems.at[0, i]) for i, (src, mid, _) in enumerate(trios)]
-    stores = [pltpu.make_async_copy(mid, dst, sems.at[1, i]) for i, (_, mid, dst) in enumerate(trios)]
-    for load in loads:
-        load.start()
-    for load, store in zip(loads, stores):
-        load.wait()
-        store.start()
-    for store in stores:
-        store.wait()
+def hand_over(a_ref, b_ref, c_ref, a_out, b_out, c_out, sems):
+    copies = [
+        pltpu.make_async_copy(src, dst, sems.at[i])
+        for i, (src, dst) in enumerate(((a_ref, a_out), (b_ref, b_out), (c_ref, c_out)))
+    ]
+    for copy in copies:
+        copy.start()
+    for copy in copies:
+        copy.wait()
 
 
 def shards(features, cotangent, expert_ids, gate_levels, w_in, w_out):
     tokens = features.shape[0] * lax.axis_size("ep")
     grad_scale = 1.0 / math.sqrt(2.0 * tokens / E)
     hbm = pl.BlockSpec(memory_space=pl.ANY)
+    vmem = pl.BlockSpec(memory_space=pltpu.VMEM)
     dma = pltpu.SemaphoreType.DMA
 
     def pair(*shape):
@@ -588,19 +585,19 @@
     grads = pl.pallas_call(
         functools.partial(kernel, grad_scale),
         out_shape=(
-            jax.ShapeDtypeStruct((TOK, QX), BF16),
-            jax.ShapeDtypeStruct((1, DIN, SPAN), BF16),
-            jax.ShapeDtypeStruct((1, SPAN, DOUT), BF16),
+            pltpu.VMEM((TOK, QX), BF16),
+            pltpu.VMEM((1, DIN, SPAN), BF16),
+            pltpu.VMEM((1, SPAN, DOUT), BF16),
         ),
         in_specs=[hbm] * 6,
-        out_specs=(hbm, hbm, hbm),
+        out_specs=(vmem,) * 3,
         scratch_shapes=[
             pltpu.VMEM((NZ, NC, QT, WB), BF16),
             pltpu.VMEM((NC, QT, WA), BF16),
             pltpu.VMEM((NZ, NC, 32, SPAN), BF16),
             pltpu.VMEM((NZ, G, SPAN), BF16),
             pltpu.VMEM((NZ, G, SPAN), BF16),
-            pltpu.VMEM((2, G, SPAN), BF16),
+            pltpu.VMEM((2, NX * RB, SPAN), BF16),
             pltpu.VMEM((G, WA), BF16),
             pltpu.VMEM((NZ, G, WB), BF16),
             pltpu.VMEM((NZ, G, WA), BF16),
@@ -622,14 +619,11 @@
             pltpu.VMEM((2, 3, SPAN, 1024), BF16),
             pltpu.VMEM((2, 3, SPAN, 1024), BF16),
             pltpu.VMEM((NY, G, QX), BF16),
-            pltpu.VMEM((NY, 2, G, QX), BF16),
+            pltpu.VMEM((NY, 2, NX * RB, QX), BF16),
             pltpu.VMEM((NC, QT, QX), F32),
             pltpu.VMEM((NY, QT, QX), BF16),
             pltpu.VMEM((TOK, QX), BF16),
-            pltpu.VMEM((DIN, SPAN), BF16),
-            pltpu.VMEM((SPAN, DOUT), BF16),
             dma((7,)),
-            dma((4,)),
             *pair(2, 4), *pair(2, 4), *pair(8), *pair(8), *pair(1),
             *pair(8, 3), *pair(3), *pair(2, 4, NX), *pair(3, 2), *pair(2, 4, NY), *pair(2, 3), *pair(2, 3),
             *pair(E - 1, NY), *pair(3),
@@ -643,11 +637,11 @@
     return pl.pallas_call(
         hand_over,
         out_shape=tuple(jax.ShapeDtypeStruct(g.shape, g.dtype) for g in grads),
-        in_specs=[hbm] * 3,
+        in_specs=[vmem] * 3,
         out_specs=(hbm,) * 3,
-        scratch_shapes=[*(pltpu.VMEM(g.shape, g.dtype) for g in grads), dma((2, 3))],
+        scratch_shapes=[dma((3,))],
         name="hand_over",
-    )(*grads)
+    )(*(pltpu.with_memory_space_constraint(g, pltpu.VMEM) for g in grads))
 
 
 def solution(mesh):

time: 119 us -> 115 us (0.966)
  Pallas kernels: 117 us -> 114 us
    pallas_call x1, Pallas kernels: 115 us -> 113 us  [shards(): pl.pallas_call(functools.partial(kernel, grad_scale), out_shape=(pltpu.VM...]
where the time goes in v4:
time: 115 us
  Pallas kernels  114 us (99%)
    pallas_call x1, Pallas kernels, shards(): pl.pallas_call(functools.partial(kernel, grad_scale), out_shape=(pltpu.VM...  113 us

profile of v4, /device:TPU:1, one launch (start us, length us, event | category | flops | bytes accessed | tf_op | source)
XLA Modules:
  0.0 115.0 jit_solution(2568655623543368753)
XLA Ops:
  0.6 113.2 %moe_backward.1 = (bf16[256,256]{1,0:T(8,128)(2,1)S(1)}, bf16[1,1024,128]{2,1,0:T(8,128)(2,1)S(1)}, bf16[1,128,2048]{2,1,0:T(8,128)(2,1)S(1)}) custom-call(bf16[256,1024]{1,0:T(8,128)(2,1)} %x_ref.1, bf16[256,2048]{1,0:T(8,128)(2,1)} %dy_ref.1, s32[2,256]{1,0:T(2,128)} %bitcast.2, s32[2,256]{1,0:T(2,128)} %bitcast.3, bf16[1,1024,128]{2,1,0:T(8,128)(2,1)} %w1_ref.1, ...), custom_call_target="tpu_custom_call" | custom-call | flops 11299999744 | bytes 5000000 | tf_op jit(solution)/shard_map/moe_backward/pallas_call | solution.py:585
  113.9 1.0 hand_over.1
